TPU v7x, 128 devices: a whole 4x4x4 slice. The times are simulated.
128 devices in a mesh: tiles: 8 (over z, core), rows: 16 (over y, x).
Axes of the slice: x: 4, y: 4, z: 4, core: 2. Of those that a mesh axis runs over, the one named last changes fastest.
Arguments:
- tile_values: bfloat16 [128, 8, 1024, 1024], P(('tiles', 'rows')), may hold values from -6 to 6
- tile_coords: int32 [128, 8, 4], P(('tiles', 'rows')), may hold values from 0 to 191, as said below
- tile_count: int32 [128], P(('tiles', 'rows')), may hold values from 4 to 8, as said below
- factors: float32 [4, 6144, 256], P(None, 'rows'), may hold values from -3 to 3
Outputs:
- updated: float32 [4, 6144, 256], P(None, 'rows')
Inputs may be any that keep to these rules, and one draw needn't show every extreme that they name: `tile_coords`: over the live slots of one device, the four modes together name blocks of one row owner (block index // 12) at most 4 times; on every device some owner is named exactly 4 times. The same block may appear in several tiles. Slot 0 is always live. Slots from tile_count[d] on are ignored; some device has all slots live.
All inputs are finite; a program needn't handle non-finite values.
Results may differ from a plain program's by a relative error of at most 0.0033.
Values may be sent and summed in bfloat16 or wider, within the bound.
No kernel may reach another device: no remote copies, remote signals or barrier semaphores. Data moves between devices by JAX's collectives and lax.ppermute only.
A program may use at most 128 MiB of HBM per device.

v0:
```python
import jax
import jax.numpy as jnp
from jax import lax
from jax.sharding import PartitionSpec as P

TILE = 32


step_size = 0.02


def tile_grads(tile_block, blocks):
    widened = blocks.astype(jnp.float32)
    mode_one, mode_two, mode_three, mode_four = (widened[0], widened[1], widened[2], widened[3])
    tile_edge = mode_one.shape[0]
    pair_ab = (
        (mode_one[:, None, :] * mode_two[None, :, :])
        .reshape(tile_edge * tile_edge, -1)
        .astype(jnp.bfloat16)
    )
    pair_cd = (
        (mode_three[:, None, :] * mode_four[None, :, :])
        .reshape(tile_edge * tile_edge, -1)
        .astype(jnp.bfloat16)
    )
    model_values = lax.dot_general(
        pair_ab, pair_cd, (((1,), (1,)), ((), ())), preferred_element_type=jnp.float32
    )
    misfit = jnp.clip(model_values - tile_block.astype(jnp.float32), -1.0, 1.0).astype(jnp.bfloat16)
    left_terms = jnp.dot(misfit, pair_cd, preferred_element_type=jnp.float32).reshape(
        tile_edge, tile_edge, -1
    )
    right_terms = lax.dot_general(
        misfit, pair_ab, (((0,), (0,)), ((), ())), preferred_element_type=jnp.float32
    ).reshape(tile_edge, tile_edge, -1)
    grad_one = jnp.sum(left_terms * mode_two[None, :, :], axis=1)
    grad_two = jnp.sum(left_terms * mode_one[:, None, :], axis=0)
    grad_three = jnp.sum(right_terms * mode_four[None, :, :], axis=1)
    grad_four = jnp.sum(right_terms * mode_three[:, None, :], axis=0)
    return jnp.stack([grad_one, grad_two, grad_three, grad_four])


def on_device(tile_values, tile_coords, tile_count, factors):
    tile_stack = tile_values[0]
    coords = tile_coords[0]
    live_count = tile_count[0]
    slot_total = coords.shape[0]
    row_peers = lax.axis_size("rows")
    local_blocks = factors.shape[1] // TILE
    narrow = factors.astype(jnp.bfloat16)
    row_index = coords[:, :, None] * TILE + jnp.arange(TILE)[None, None, :]
    mode_index = jnp.arange(4)[None, :, None]
    everything = lax.all_gather(narrow, "rows", axis=1, tiled=True)
    blocks = everything[mode_index, row_index]

    def accumulate(slot_idx, running):
        gradient = tile_grads(tile_stack[slot_idx], blocks[slot_idx])
        return lax.dynamic_update_index_in_dim(running, gradient, slot_idx, 0)

    grad_blocks = lax.fori_loop(
        0, live_count, accumulate, jnp.zeros((slot_total, 4, TILE, factors.shape[2]), jnp.float32)
    )
    dense_grads = jnp.zeros((4, row_peers * local_blocks * TILE, factors.shape[2]), jnp.float32)
    dense_grads = dense_grads.at[mode_index, row_index].add(grad_blocks)
    partial_sum = lax.psum_scatter(dense_grads, "rows", scatter_dimension=1, tiled=True)
    total_grad = lax.psum(partial_sum, "tiles")
    return factors - step_size * total_grad


def solution(mesh):
    return jax.shard_map(
        on_device,
        mesh=mesh,
        in_specs=(
            P(("tiles", "rows"), None, None, None),
            P(("tiles", "rows"), None, None),
            P(("tiles", "rows")),
            P(None, "rows", None),
        ),
        out_specs=P(None, "rows", None),
        check_vma=False,
    )
```

profile of v0, /device:TPU:1, one launch (start us, length us, event | category | flops | bytes accessed | tf_op | source)
XLA Modules:
  0.0 438.0 jit_solution(16782204517564997862)
XLA Ops:
  6.5 2.4 convert_element_type.48
  9.6 93.0 %all-gather.2.cloned.1.call-done = bf16[4,6144,256]{2,1,0:T(8,128)(2,1)} async-done(((bf16[4,384,256]{2,1,0:T(8,128)(2,1)}), bf16[4,6144,256]{2,1,0:T(8,128)(2,1)}) %all-gather.2.cloned.1.call-update) | async-done | bytes 12582928 | tf_op jit(solution)/shard_map/all_gather | solution.py:53
  102.6 13.2 %gather_fusion = bf16[1024,256]{1,0:T(8,128)(2,1)S(1)} fusion(bf16[4,6144,256]{2,1,0:T(8,128)(2,1)} %all-gather.2.cloned.1.call-done, s32[1024]{0:T(1024)S(1)} %reshape.83), kind=kCustom, calls=%fused_computation | custom fusion | bytes 1056768 | tf_op jit(solution)/shard_map/gather | solution.py:54
  115.8 1.1 broadcast_in_dim.12
  116.9 68.3 %while.10 = (s32[]{:T(128)}, f32[8,4,32,256]{3,2,1,0:T(8,128)}, s32[]{:T(128)}, bf16[8,4,32,256]{3,2,1,0:T(8,128)(2,1)S(1)}, bf16[8,1024,1024]{2,1,0:T(8,128)(2,1)}, /*index=5*/s32[]{:T(128)}, s32[]{:T(128)}, s32[]{:T(128)}) while((s32[]{:T(128)}, f32[8,4,32,256]{3,2,1,0:T(8,128)}, s32[]{:T(128)}, bf16[8,4,32,256]{3,2,1,0:T(8,128)(2,1)S(1)}, ...), condition=%wide.region_5.6_spmd, body=%wide.region_0.5_spmd.sunk | while | flops 1618051072 | bytes 16842892 | solution.py:60
  117.9 2.3 fusion.25
  121.0 2.6 copy.10
  123.6 2.3 multiply_reduce_fusion.7
  127.6 2.3 fusion.25
  130.0 0.7 multiply_reduce_fusion.8
  130.7 2.6 copy.10
  133.3 2.3 multiply_reduce_fusion.7
  137.3 2.3 fusion.25
  140.4 2.6 copy.10
  142.9 2.3 multiply_reduce_fusion.7
  146.9 2.3 fusion.25
  150.0 2.6 copy.10
  152.6 2.3 multiply_reduce_fusion.7
  156.6 2.3 fusion.25
  158.9 0.7 multiply_reduce_fusion.8
  159.7 2.6 copy.10
  162.3 2.3 multiply_reduce_fusion.7
  166.3 2.3 fusion.25
  169.3 2.6 copy.10
  171.9 2.3 multiply_reduce_fusion.7
  175.9 2.3 fusion.25
  179.0 2.6 copy.10
  181.6 2.3 multiply_reduce_fusion.7
  185.2 16.4 %scatter_custom_fusion = f32[24576,256]{1,0:T(8,128)} fusion(s32[1024]{0:T(1024)S(1)} %reshape.89, f32[1024,256]{1,0:T(8,128)} %bitcast.93, f32[]{:T(128)} %constant.3.clone.1), kind=kCustom, calls=%fused_computation.18 | custom fusion | flops 262144 | bytes 25166336
  201.7 162.5 %reduce-scatter.2.cloned.1.call-done = f32[4,384,256]{2,1,0:T(8,128)} async-done(((f32[4,6144,256]{2,1,0:T(8,128)}), f32[4,384,256]{2,1,0:T(8,128)}) %reduce-scatter.2.cloned.1.call-update) | async-done | bytes 1572880 | tf_op jit(solution)/shard_map/reduce_scatter | solution.py:65
  364.2 64.4 %all-reduce.2.cloned.1.call-done = f32[4,384,256]{2,1,0:T(8,128)} async-done(((f32[4,384,256]{2,1,0:T(8,128)}), f32[4,384,256]{2,1,0:T(8,128)}) %all-reduce.2.cloned.1.call-update) | async-done | bytes 1572880 | tf_op jit(solution)/shard_map/psum | solution.py:66
  428.7 2.8 multiply_subtract_fusion
  (56 shorter events, 11.3 us)
Async XLA Ops:
  6.5 2.7 copy-start.3
  6.5 2.8 copy-start.2
  6.5 2.5 copy-start.1
  6.5 96.1 %all-gather.2.cloned.1.call-start = ((), (), s32[]{:S(2)}) async-start(), calls=%async_computation.1 | async-start | bytes 13369344 | tf_op jit(solution)/shard_map/all_gather | solution.py:53
  8.9 355.3 %reduce-scatter.2.cloned.1.call-start = ((), (), s32[]{:S(2)}) async-start(), calls=%async_computation.2 | async-start | bytes 26738688 | tf_op jit(solution)/shard_map/reduce_scatter | solution.py:65
  201.7 227.0 %copy-start = (f32[4,384,256]{2,1,0:T(8,128)S(1)}, f32[4,384,256]{2,1,0:T(8,128)}, u32[]{:S(2)}) copy-start(f32[4,384,256]{2,1,0:T(8,128)} %param.9) | copy-start | bytes 4718596
  201.7 227.0 %all-reduce.2.cloned.1.call-start = ((), (), s32[]{:S(2)}) async-start(), calls=%async_computation.3 | async-start | bytes 3145728 | tf_op jit(solution)/shard_map/psum | solution.py:66
Sparse Core Ops, SparseCore 0:
  9.5 93.0 all-gather.1
  201.8 162.3 reduce-scatter.1
  366.6 62.0 all-reduce.1
where the time goes:
time: 440 us; the launch traced here: 438 us
  waiting for transfers between devices  320 us (73%)
  matrix products  37.7 us (9%)
  local copies, waits for them, and re-layouts  32.7 us (7%)
  other arithmetic  28.7 us (7%)
  between operations  13.2 us (3%)
  loops' own time  5.59 us (1%)
    reduce_scatter x1, waiting for transfers between devices, on_device(): lax.psum_scatter(dense_grads, 'rows', scatter_dimension=1, tiled=True)  162 us
    all_gather x1, waiting for transfers between devices, on_device(): everything = lax.all_gather(narrow, 'rows', axis=1, tiled=True)  93 us
    psum x1, waiting for transfers between devices, on_device(): total_grad = lax.psum(partial_sum, 'tiles')  64.4 us
    dot_general x7, local copies, waits for them, and re-layouts, tile_grads(): lax.dot_general(misfit, pair_ab, (((0,), (0,)), ((), ())), preferred_elem...  18 us
    unnamed x4, other arithmetic  16.6 us
    dot_general x7, matrix products, tile_grads(): lax.dot_general(pair_ab, pair_cd, (((1,), (1,)), ((), ())), preferred_ele...  16.4 us
    dot_general x7, matrix products, tile_grads(): lax.dot_general(misfit, pair_ab, (((0,), (0,)), ((), ())), preferred_elem...  16.2 us
    gather x1, local copies, waits for them, and re-layouts, on_device(): blocks = everything[mode_index, row_index]  13.2 us
  transfers between devices with their start and end apart: 3, of which 3 were waited for; matrix products, arithmetic and copies ran while one was open for 0% of the time, Pallas kernels for 0%

commit v1 on v0

v1 whole, which is shorter than its diff:
```python
import functools

import jax
import jax.numpy as jnp
from jax import lax
from jax.experimental import pallas as pl
from jax.experimental.pallas import tpu as pltpu
from jax.sharding import PartitionSpec as P

TILE = 32
CAP = 4
EDGE = TILE * TILE
LANES = 128

step_size = 0.02

VMEM = pl.BlockSpec(memory_space=pltpu.VMEM)
SMEM = pl.BlockSpec(memory_space=pltpu.SMEM)


def request_kernel(owners, blk_dev, coords, count, wanted, slots, used):
    lines = (owners, LANES)
    row = lax.broadcasted_iota(jnp.int32, lines, 0)
    lane = lax.broadcasted_iota(jnp.int32, lines, 1)
    for owner in range(owners):
        used[owner] = 0

    def tile(slot, table):
        for mode in range(4):
            block = coords[mode, slot]
            owner = block // blk_dev
            rank = used[owner]
            used[owner] = rank + 1
            slots[slot * 4 + mode] = owner * CAP + rank
            local = mode * blk_dev + block - owner * blk_dev
            table = jnp.where((row == owner) & (lane == rank), local, table)
        return table

    table = lax.fori_loop(0, count[0], tile, jnp.full(lines, -1, jnp.int32))
    for owner in range(owners):
        wanted[owner] = jnp.broadcast_to(table[owner : owner + 1], wanted.shape[1:])


def serve_kernel(peers, asked, factors, sent, table):
    lane = lax.broadcasted_iota(jnp.int32, table.shape, 1)
    listed = jnp.full(table.shape, -1, jnp.int32)
    for peer in range(peers):
        for rank in range(CAP):
            local = asked[peer, 0, rank]
            listed = jnp.where(lane == peer * CAP + rank, local, listed)
            sent[peer, rank * TILE : (rank + 1) * TILE, :] = factors[jnp.maximum(local, 0)].astype(
                jnp.bfloat16
            )
    table[...] = listed


def tile_kernel(
    owners, parts, chunk, count, slots, blocks, tiles, out, values, misfit, pair_ab, pair_cd, grads, sem
):
    live = count[0]
    f32, bf16 = jnp.float32, jnp.bfloat16
    rank = blocks.shape[-1]

    def fetch(slot):
        place = lax.rem(slot, 2)
        return pltpu.make_async_copy(tiles.at[slot], values.at[place], sem.at[place])

    fetch(0).start()
    grads[...] = jnp.zeros_like(grads)

    def tile(slot, carry):
        @pl.when(slot + 1 < live)
        def _():
            fetch(slot + 1).start()

        names = [slots[slot * 4 + mode] for mode in range(4)]
        one, two, three, four = [
            blocks[pl.ds(pl.multiple_of(name * TILE, TILE), TILE), :].astype(f32) for name in names
        ]
        for i in range(TILE):
            at = slice(i * TILE, (i + 1) * TILE)
            pair_ab[at, :] = (one[i : i + 1] * two).astype(bf16)
            pair_cd[at, :] = (three[i : i + 1] * four).astype(bf16)
        fetch(slot).wait()
        place = lax.rem(slot, 2)
        outer = chunk // TILE
        grad_one, grad_two = [], jnp.zeros((TILE, rank), f32)
        for at in range(0, EDGE, chunk):
            model = lax.dot_general(
                pair_ab[at : at + chunk, :],
                pair_cd[...],
                (((1,), (1,)), ((), ())),
                preferred_element_type=f32,
            )
            off = jnp.clip(model - values[place, at : at + chunk, :].astype(f32), -1.0, 1.0).astype(bf16)
            misfit[at : at + chunk, :] = off
            left = jnp.dot(off, pair_cd[...], preferred_element_type=f32).reshape(outer, TILE, rank)
            grad_one.append(jnp.sum(left * two[None], axis=1))
            for i in range(outer):
                first = at // TILE + i
                grad_two = grad_two + left[i] * one[first : first + 1]
        grad_three, grad_four = [], jnp.zeros((TILE, rank), f32)
        for at in range(0, EDGE, chunk):
            right = lax.dot_general(
                misfit[:, at : at + chunk],
                pair_ab[...],
                (((0,), (0,)), ((), ())),
                preferred_element_type=f32,
            ).reshape(outer, TILE, rank)
            grad_three.append(jnp.sum(right * four[None], axis=1))
            for k in range(outer):
                first = at // TILE + k
                grad_four = grad_four + right[k] * three[first : first + 1]
        grads[names[0]] = jnp.concatenate(grad_one, 0)
        grads[names[1]] = grad_two
        grads[names[2]] = jnp.concatenate(grad_three, 0)
        grads[names[3]] = grad_four
        return carry

    lax.fori_loop(0, live, tile, 0)
    height = TILE // parts
    for owner in range(owners):
        for part in range(parts):
            out[part * owners + owner] = jnp.concatenate(
                [
                    grads[owner * CAP + place, part * height : (part + 1) * height, :]
                    for place in range(CAP)
                ],
                0,
            ).astype(bf16)


def add_kernel(peers, layer, table_0, table_1, table_2, table_3, came, total, *sums):
    tables = (table_0, table_1, table_2, table_3)
    height = total.shape[0] // sums[0].shape[0]
    for acc in sums:
        acc[...] = jnp.zeros_like(acc)
    for back, table in enumerate(tables):
        source = lax.rem(layer[0] + len(tables) - back, len(tables))

        def peer_step(peer, carry, table=table, source=source):
            message = came[source * peers + peer].astype(jnp.float32)
            for rank, acc in enumerate(sums):
                local = jnp.maximum(table[0, peer * CAP + rank], 0)
                acc[local] += message[rank * height : (rank + 1) * height]
            return carry

        lax.fori_loop(0, peers, peer_step, 0, unroll=4)
    summed = sums[0][...] + sums[1][...] + sums[2][...] + sums[3][...]
    total[...] = summed.reshape(total.shape).astype(total.dtype)


def update_kernel(layer, factors, *refs):
    own, other, out = refs[:4], refs[4:8], refs[8]
    parts = len(own)
    height = TILE // parts
    for back in range(parts):
        source = lax.rem(layer[0] + parts - back, parts)
        at = pl.ds(pl.multiple_of(source * height, height), height)
        gradient = own[back][...].astype(jnp.float32) + other[back][...].astype(jnp.float32)
        gradient = gradient.reshape(out.shape[0], height, -1)
        out[:, at, :] = factors[:, at, :] - step_size * gradient


def on_device(layers, owners, tile_values, tile_coords, tile_count, factors):
    blk_dev = factors.shape[1] // TILE
    rank = factors.shape[2]
    held = 4 * blk_dev
    slot_total = tile_values.shape[1]
    factor_blocks = factors.reshape(held, TILE, rank)
    layer = (lax.axis_index("tiles") // 2).astype(jnp.int32).reshape(1)
    bf16, f32, i32 = jnp.bfloat16, jnp.float32, jnp.int32

    wanted, slots = pl.pallas_call(
        functools.partial(request_kernel, owners, blk_dev),
        out_shape=(
            jax.ShapeDtypeStruct((owners, 8, LANES), i32),
            jax.ShapeDtypeStruct((slot_total * 4,), i32),
        ),
        in_specs=[SMEM, SMEM],
        out_specs=(VMEM, SMEM),
        scratch_shapes=[pltpu.SMEM((owners,), i32)],
        name="requests",
    )(tile_coords[0].T, tile_count)
    asked = lax.all_to_all(wanted, "rows", 0, 0)

    sent, table = pl.pallas_call(
        functools.partial(serve_kernel, owners),
        out_shape=(
            jax.ShapeDtypeStruct((owners, CAP * TILE, rank), bf16),
            jax.ShapeDtypeStruct((8, LANES), i32),
        ),
        in_specs=[SMEM, VMEM],
        out_specs=(VMEM, VMEM),
        name="serve",
    )(asked, factor_blocks)
    blocks = lax.all_to_all(sent, "rows", 0, 0).reshape(owners * CAP * TILE, rank)

    def round_trip(back):
        size = 2 * layers
        return [(i, (i + 2 * back) % size) for i in range(size)]

    tables = [table] + [lax.ppermute(table, "tiles", round_trip(back)) for back in range(1, layers)]

    flops = 3 * 2 * EDGE * EDGE * rank * slot_total
    messages = pl.pallas_call(
        functools.partial(tile_kernel, owners, layers, 256),
        out_shape=jax.ShapeDtypeStruct((layers * owners, CAP * TILE // layers, rank), bf16),
        in_specs=[SMEM, SMEM, VMEM, pl.BlockSpec(memory_space=pl.ANY)],
        out_specs=VMEM,
        scratch_shapes=[
            pltpu.VMEM((2, EDGE, EDGE), bf16),
            pltpu.VMEM((EDGE, EDGE), bf16),
            pltpu.VMEM((EDGE, rank), bf16),
            pltpu.VMEM((EDGE, rank), bf16),
            pltpu.VMEM((owners * CAP, TILE, rank), f32),
            pltpu.SemaphoreType.DMA((2,)),
        ],
        compiler_params=pltpu.CompilerParams(vmem_limit_bytes=40 << 20),
        cost_estimate=pl.CostEstimate(
            flops=flops, bytes_accessed=2 * EDGE * EDGE * slot_total, transcendentals=0
        ),
        name="tiles",
    )(tile_count, slots, blocks, tile_values[0])

    same_core = [
        [t * owners + r for t in range(core, 2 * layers, 2) for r in range(owners)] for core in range(2)
    ]
    came = lax.all_to_all(messages, ("tiles", "rows"), 0, 0, axis_index_groups=same_core)

    height = TILE // layers
    partial = pl.pallas_call(
        functools.partial(add_kernel, owners),
        out_shape=jax.ShapeDtypeStruct((held * height, rank), bf16),
        in_specs=[SMEM] * (1 + layers) + [VMEM],
        out_specs=VMEM,
        scratch_shapes=[pltpu.VMEM((held, height, rank), f32)] * CAP,
        name="add",
    )(layer, *tables, came)

    own = [partial] + [lax.ppermute(partial, "tiles", round_trip(back)) for back in range(1, layers)]
    pair = [(i, i ^ 1) for i in range(2 * layers)]
    other = [lax.ppermute(piece, "tiles", pair) for piece in own]

    updated = pl.pallas_call(
        update_kernel,
        out_shape=jax.ShapeDtypeStruct(factor_blocks.shape, f32),
        in_specs=[SMEM] + [VMEM] * 9,
        out_specs=VMEM,
        name="update",
    )(layer, factor_blocks, *own, *other)
    return updated.reshape(factors.shape)


def solution(mesh):
    layers, owners = mesh.shape["tiles"] // 2, mesh.shape["rows"]
    return jax.shard_map(
        functools.partial(on_device, layers, owners),
        mesh=mesh,
        in_specs=(
            P(("tiles", "rows"), None, None, None),
            P(("tiles", "rows"), None, None),
            P(("tiles", "rows")),
            P(None, "rows", None),
        ),
        out_specs=P(None, "rows", None),
        check_vma=False,
    )
```

time: 440 us -> 104 us (0.24)
  waiting for transfers between devices: 320 us -> 13 us
  matrix products: 37.7 us -> 0 us
  blocking collectives: 0 us -> 33.3 us
  local copies, waits for them, and re-layouts: 32.7 us -> 1.67 us
  starting transfers between devices: 0.09 us -> 28.9 us
  other arithmetic: 28.7 us -> 0 us
  Pallas kernels: 0 us -> 26.2 us
  between operations: 13.2 us -> 0.77 us
  loops' own time: 5.59 us -> 0 us
    reduce_scatter x1 -> x0, waiting for transfers between devices: 162 us -> none  [on_device(): lax.psum_scatter(dense_grads, 'rows', scatter_dimension=1, tiled=True)]
    all_gather x1 -> x0, waiting for transfers between devices: 93 us -> none  [on_device(): everything = lax.all_gather(narrow, 'rows', axis=1, tiled=True)]
    psum x1 -> x0, waiting for transfers between devices: 64.4 us -> none  [on_device(): total_grad = lax.psum(partial_sum, 'tiles')]
    dot_general x21 -> x0, matrix products: 37.7 us -> none  [the longest x7 16.4 us: tile_grads(): lax.dot_general(pair_ab, pair_cd, (((1,), (1,)), ((), ())), preferred_ele...]
    all_to_all x0 -> x2, blocking collectives: none -> 33.3 us  [the longest x1 19.1 us: on_device(): lax.all_to_all(sent, 'rows', 0, 0).reshape(owners * CAP * TILE, rank)]
    pallas_call x0 -> x5, Pallas kernels: none -> 26.2 us  [the longest x1 15.9 us: on_device(): pl.pallas_call(functools.partial(tile_kernel, owners, layers, 256), out_s...]
    ppermute x0 -> x10, starting transfers between devices: none -> 18.1 us  [the longest x4 13.1 us: on_device(): other = [lax.ppermute(piece, 'tiles', pair) for piece in own]]
    dot_general x7 -> x0, local copies, waits for them, and re-layouts: 18 us -> none  [tile_grads(): lax.dot_general(misfit, pair_ab, (((0,), (0,)), ((), ())), preferred_elem...]
  transfers between devices with their start and end apart: 3 -> 11, of which waited for: 3 -> 4; matrix products, arithmetic and copies ran while one was open for 0% -> 0% of each run, Pallas kernels for 0% -> 0%
where the time goes in v1:
time: 104 us
  blocking collectives  33.3 us (32%)
  starting transfers between devices  28.9 us (28%)
  Pallas kernels  26.2 us (25%)
  waiting for transfers between devices  13 us (12%)
  local copies, waits for them, and re-layouts  1.67 us (2%)
    all_to_all x1, blocking collectives, on_device(): lax.all_to_all(sent, 'rows', 0, 0).reshape(owners * CAP * TILE, rank)  19.1 us
    pallas_call x1, Pallas kernels, on_device(): pl.pallas_call(functools.partial(tile_kernel, owners, layers, 256), out_s...  15.9 us
    all_to_all x1, blocking collectives, on_device(): asked = lax.all_to_all(wanted, 'rows', 0, 0)  14.2 us
    ppermute x4, starting transfers between devices, on_device(): other = [lax.ppermute(piece, 'tiles', pair) for piece in own]  13.1 us
    all_to_all x1, starting transfers between devices, on_device(): lax.all_to_all(messages, ('tiles', 'rows'), 0, 0, axis_index_groups=same_...  10.8 us
    all_to_all x1, waiting for transfers between devices, on_device(): lax.all_to_all(messages, ('tiles', 'rows'), 0, 0, axis_index_groups=same_...  8.63 us
    ppermute x3, starting transfers between devices, on_device(): lax.ppermute(table, 'tiles', round_trip(back))  3.54 us
    pallas_call x1, Pallas kernels, on_device(): pl.pallas_call(update_kernel, out_shape=jax.ShapeDtypeStruct(factor_block...  3.35 us
  transfers between devices with their start and end apart: 11, of which 4 were waited for; matrix products, arithmetic and copies ran while one was open for 0% of the time, Pallas kernels for 0%

profile of v1, /device:TPU:1, one launch (start us, length us, event | category | flops | bytes accessed | tf_op | source)
XLA Modules:
  0.0 103.9 jit_solution(5866433420933149639)
XLA Ops:
  0.7 1.6 %requests.1 = (s32[16,8,128]{2,1,0:T(8,128)}, s32[32]{0:T(128)}) custom-call(s32[4,8]{1,0:T(4,128)} %bitcast.11, s32[1]{0:T(128)S(6)} %copy.5.count), custom_call_target="tpu_custom_call" | custom-call | tf_op jit(solution)/shard_map/requests/pallas_call | solution.py:174
  2.2 14.2 %all_to_all.15.asked = s32[16,8,128]{2,1,0:T(8,128)} all-to-all(s32[16,8,128]{2,1,0:T(8,128)} %get-tuple-element.9), channel_id=1, replica_groups=mesh['tiles'=8,'rows'=16] {'rows'}, dimensions={0} | all-to-all | bytes 131072 | tf_op jit(solution)/shard_map/all_to_all | solution.py:185
  16.4 2.8 %serve.1 = (bf16[16,128,256]{2,1,0:T(8,128)(2,1)}, s32[8,128]{1,0:T(8,128)}) custom-call(s32[16,8,128]{2,1,0:T(8,128)} %all_to_all.15.asked, f32[48,32,256]{2,1,0:T(8,128)} %bitcast.9), custom_call_target="tpu_custom_call" | custom-call | tf_op jit(solution)/shard_map/serve/pallas_call | solution.py:187
  19.2 19.1 %all_to_all.16 = bf16[16,128,256]{2,1,0:T(8,128)(2,1)S(1)} all-to-all(bf16[16,128,256]{2,1,0:T(8,128)(2,1)} %get-tuple-element.12), channel_id=1, replica_groups=mesh['tiles'=8,'rows'=16] {'rows'}, dimensions={0} | all-to-all | bytes 2097152 | tf_op jit(solution)/shard_map/all_to_all | solution.py:197
  38.4 15.9 %tiles.1 = bf16[64,32,256]{2,1,0:T(8,128)(2,1)} custom-call(s32[1]{0:T(128)S(6)} %copy.5.count, s32[32]{0:T(128)S(1)} %copy-done, bf16[2048,256]{1,0:T(8,128)(2,1)S(1)} %bitcast.8, bf16[8,1024,1024]{2,1,0:T(8,128)(2,1)} %bitcast.12), custom_call_target="tpu_custom_call" | custom-call | flops 12884901888 | bytes 16777216 | tf_op jit(solution)/shard_map/tiles/pallas_call | solution.py:206
  54.2 10.8 %all-to-all-start.2 = ((bf16[64,32,256]{2,1,0:T(8,128)(2,1)}), bf16[64,32,256]{2,1,0:T(8,128)(2,1)S(1)}, u32[]{:S(2)}, u32[]{:S(2)}) async-start(bf16[64,32,256]{2,1,0:T(8,128)(2,1)} %tiles.1), calls=%async_computation.2 | async-start | bytes 2097152 | tf_op jit(solution)/shard_map/all_to_all | solution.py:229
  65.1 0.0 copy-done.9
  65.1 2.5 %collective-permute-start.2 = (s32[8,128]{1,0:T(8,128)S(1)}, s32[8,128]{1,0:T(8,128)S(1)}, u32[]{:S(2)}, u32[]{:S(2)}) collective-permute-start(s32[8,128]{1,0:T(8,128)S(1)} %copy-done.9), channel_id=1, source_target_pairs={{0,96},{16,112},{32,0},{48,16},{64,32},{80,48},{96,64},{112,80},{1... | collective-permute-start | bytes 12296 | tf_op jit(solution)/shard_map/ppermute | solution.py:203
  67.6 0.4 collective-permute-start.1
  68.0 0.7 collective-permute-start
  68.6 0.0 collective-permute-done.2.table_3
  68.6 3.2 %collective-permute-done.1.table_2 = s32[8,128]{1,0:T(8,128)S(1)} collective-permute-done((s32[8,128]{1,0:T(8,128)S(1)}, s32[8,128]{1,0:T(8,128)S(1)}, u32[]{:S(2)}, u32[]{:S(2)}) %collective-permute-start.1) | collective-permute-done | bytes 4128 | tf_op jit(solution)/shard_map/ppermute | solution.py:203
  71.8 0.1 collective-permute-done.table_1
  72.0 8.6 %all-to-all-done.2.came = bf16[64,32,256]{2,1,0:T(8,128)(2,1)S(1)} async-done(((bf16[64,32,256]{2,1,0:T(8,128)(2,1)}), bf16[64,32,256]{2,1,0:T(8,128)(2,1)S(1)}, u32[]{:S(2)}, u32[]{:S(2)}) %all-to-all-start.2) | async-done | bytes 1048608 | tf_op jit(solution)/shard_map/all_to_all | solution.py:229
  80.6 1.0 copy-done.1
  81.6 2.6 %add.2.refs_0_ = bf16[384,256]{1,0:T(8,128)(2,1)} custom-call(s32[1]{0:T(128)} %bitcast.layer, s32[8,128]{1,0:T(8,128)} %get-tuple-element.10.table_0, s32[8,128]{1,0:T(8,128)} %copy-done.12, s32[8,128]{1,0:T(8,128)} %copy-done.11, s32[8,128]{1,0:T(8,128)} %copy-done.10, bf16[64,32,256]{2,1,0:T(8,128)(2,1)} %copy-done.1), custom_call_target="tpu_custom_call" | custom-call | tf_op jit(solution)/shard_map/add/pallas_call | solution.py:232
  84.2 0.6 collective-permute-start.5
  84.8 0.8 collective-permute-start.4
  85.6 0.0 collective-permute-start.3
  85.7 5.3 %collective-permute-start.6 = (bf16[384,256]{1,0:T(8,128)(2,1)}, bf16[384,256]{1,0:T(8,128)(2,1)S(1)}, u32[]{:S(2)}, u32[]{:S(2)}) collective-permute-start(bf16[384,256]{1,0:T(8,128)(2,1)} %add.2.refs_0_), channel_id=1, source_target_pairs={{0,16},{16,0},{32,48},{48,32},{64,80},{80,64},{96,112},{112,96},{1... | collective-permute-start | bytes 589832 | tf_op jit(solution)/shard_map/ppermute | solution.py:243
  91.0 0.0 collective-permute-done.5.refs_3_
  91.0 3.4 %collective-permute-start.9 = (bf16[384,256]{1,0:T(8,128)(2,1)S(1)}, bf16[384,256]{1,0:T(8,128)(2,1)S(1)}, u32[]{:S(2)}, u32[]{:S(2)}) collective-permute-start(bf16[384,256]{1,0:T(8,128)(2,1)S(1)} %collective-permute-done.5.refs_3_), channel_id=1, source_target_pairs={{0,16},{16,0},{32,48},{48,32},{64,80},{80,64},{96,112},{112,96},{1... | collective-permute-start | bytes 589832 | tf_op jit(solution)/shard_map/ppermute | solution.py:243
  94.4 0.0 collective-permute-done.4.refs_2_
  94.4 2.4 %collective-permute-start.8 = (bf16[384,256]{1,0:T(8,128)(2,1)S(1)}, bf16[384,256]{1,0:T(8,128)(2,1)S(1)}, u32[]{:S(2)}, u32[]{:S(2)}) collective-permute-start(bf16[384,256]{1,0:T(8,128)(2,1)S(1)} %collective-permute-done.4.refs_2_), channel_id=1, source_target_pairs={{0,16},{16,0},{32,48},{48,32},{64,80},{80,64},{96,112},{112,96},{1... | collective-permute-start | bytes 589832 | tf_op jit(solution)/shard_map/ppermute | solution.py:243
  96.8 0.0 collective-permute-done.3.refs_1_
  96.8 2.0 %collective-permute-start.7 = (bf16[384,256]{1,0:T(8,128)(2,1)S(1)}, bf16[384,256]{1,0:T(8,128)(2,1)S(1)}, u32[]{:S(2)}, u32[]{:S(2)}) collective-permute-start(bf16[384,256]{1,0:T(8,128)(2,1)S(1)} %collective-permute-done.3.refs_1_), channel_id=1, source_target_pairs={{0,16},{16,0},{32,48},{48,32},{64,80},{80,64},{96,112},{112,96},{1... | collective-permute-start | bytes 589832 | tf_op jit(solution)/shard_map/ppermute | solution.py:243
  98.8 0.0 collective-permute-done.6.refs_4_
  98.8 0.0 collective-permute-done.9.refs_7_
  98.8 0.0 collective-permute-done.8.refs_6_
  98.8 1.0 collective-permute-done.7.refs_5_
  99.9 0.7 copy-done.8
  100.6 3.3 %update.1 = f32[48,32,256]{2,1,0:T(8,128)} custom-call(s32[1]{0:T(128)} %bitcast.layer, f32[48,32,256]{2,1,0:T(8,128)} %bitcast.10, bf16[384,256]{1,0:T(8,128)(2,1)} %add.2.refs_0_, bf16[384,256]{1,0:T(8,128)(2,1)} %copy-done.4, bf16[384,256]{1,0:T(8,128)(2,1)} %copy-done.3, bf16[384,256]{1,0:T(8,128)(2,1)} %copy-done.2, bf16[384,256]{1,0:T(8,128)(2,1)} %copy-done.5, ...), custom_call_target="tpu_custom_call" | custom-call | tf_op jit(solution)/shard_map/update/pallas_call | solution.py:245
  (23 shorter events, 0.0 us)
Async XLA Ops:
  16.4 22.0 %copy-start = (s32[32]{0:T(128)S(1)}, s32[32]{0:T(128)}, u32[]{:S(2)}) copy-start(s32[32]{0:T(128)} %get-tuple-element.11.slots) | copy-start | bytes 388
  54.2 10.8 %copy-start.9 = (s32[8,128]{1,0:T(8,128)S(1)}, s32[8,128]{1,0:T(8,128)}, u32[]{:S(2)}) copy-start(s32[8,128]{1,0:T(8,128)} %get-tuple-element.10.table_0) | copy-start | bytes 12292
  54.2 26.4 %all-to-all-start.2 = ((bf16[64,32,256]{2,1,0:T(8,128)(2,1)}), bf16[64,32,256]{2,1,0:T(8,128)(2,1)S(1)}, u32[]{:S(2)}, u32[]{:S(2)}) async-start(bf16[64,32,256]{2,1,0:T(8,128)(2,1)} %tiles.1), calls=%async_computation.2 | async-start | bytes 2097152 | tf_op jit(solution)/shard_map/all_to_all | solution.py:229
  65.1 3.5 %collective-permute-start.2 = (s32[8,128]{1,0:T(8,128)S(1)}, s32[8,128]{1,0:T(8,128)S(1)}, u32[]{:S(2)}, u32[]{:S(2)}) collective-permute-start(s32[8,128]{1,0:T(8,128)S(1)} %copy-done.9), channel_id=1, source_target_pairs={{0,96},{16,112},{32,0},{48,16},{64,32},{80,48},{96,64},{112,80},{1... | collective-permute-start | bytes 12296 | tf_op jit(solution)/shard_map/ppermute | solution.py:203
  67.6 4.3 %collective-permute-start.1 = (s32[8,128]{1,0:T(8,128)S(1)}, s32[8,128]{1,0:T(8,128)S(1)}, u32[]{:S(2)}, u32[]{:S(2)}) collective-permute-start(s32[8,128]{1,0:T(8,128)S(1)} %copy-done.9), channel_id=1, source_target_pairs={{0,64},{16,80},{32,96},{48,112},{64,0},{80,16},{96,32},{112,48},{1... | collective-permute-start | bytes 12296 | tf_op jit(solution)/shard_map/ppermute | solution.py:203
  68.0 4.0 %collective-permute-start = (s32[8,128]{1,0:T(8,128)S(1)}, s32[8,128]{1,0:T(8,128)S(1)}, u32[]{:S(2)}, u32[]{:S(2)}) collective-permute-start(s32[8,128]{1,0:T(8,128)S(1)} %copy-done.9), channel_id=1, source_target_pairs={{0,32},{16,48},{32,64},{48,80},{64,96},{80,112},{96,0},{112,16},{1... | collective-permute-start | bytes 12296 | tf_op jit(solution)/shard_map/ppermute | solution.py:203
  68.6 12.0 %copy-start.10 = (s32[8,128]{1,0:T(8,128)}, s32[8,128]{1,0:T(8,128)S(1)}, u32[]{:S(2)}) copy-start(s32[8,128]{1,0:T(8,128)S(1)} %collective-permute-done.2.table_3) | copy-start | bytes 12292
  71.8 8.8 %copy-start.11 = (s32[8,128]{1,0:T(8,128)}, s32[8,128]{1,0:T(8,128)S(1)}, u32[]{:S(2)}) copy-start(s32[8,128]{1,0:T(8,128)S(1)} %collective-permute-done.1.table_2) | copy-start | bytes 12292
  72.0 8.6 %copy-start.12 = (s32[8,128]{1,0:T(8,128)}, s32[8,128]{1,0:T(8,128)S(1)}, u32[]{:S(2)}) copy-start(s32[8,128]{1,0:T(8,128)S(1)} %collective-permute-done.table_1) | copy-start | bytes 12292
  80.6 1.0 copy-start.1
  84.2 6.8 %collective-permute-start.5 = (bf16[384,256]{1,0:T(8,128)(2,1)}, bf16[384,256]{1,0:T(8,128)(2,1)S(1)}, u32[]{:S(2)}, u32[]{:S(2)}) collective-permute-start(bf16[384,256]{1,0:T(8,128)(2,1)} %add.2.refs_0_), channel_id=1, source_target_pairs={{0,96},{16,112},{32,0},{48,16},{64,32},{80,48},{96,64},{112,80},{1... | collective-permute-start | bytes 589832 | tf_op jit(solution)/shard_map/ppermute | solution.py:241
  84.8 9.6 %collective-permute-start.4 = (bf16[384,256]{1,0:T(8,128)(2,1)}, bf16[384,256]{1,0:T(8,128)(2,1)S(1)}, u32[]{:S(2)}, u32[]{:S(2)}) collective-permute-start(bf16[384,256]{1,0:T(8,128)(2,1)} %add.2.refs_0_), channel_id=1, source_target_pairs={{0,64},{16,80},{32,96},{48,112},{64,0},{80,16},{96,32},{112,48},{1... | collective-permute-start | bytes 589832 | tf_op jit(solution)/shard_map/ppermute | solution.py:241
  85.6 11.1 %collective-permute-start.3 = (bf16[384,256]{1,0:T(8,128)(2,1)}, bf16[384,256]{1,0:T(8,128)(2,1)S(1)}, u32[]{:S(2)}, u32[]{:S(2)}) collective-permute-start(bf16[384,256]{1,0:T(8,128)(2,1)} %add.2.refs_0_), channel_id=1, source_target_pairs={{0,32},{16,48},{32,64},{48,80},{64,96},{80,112},{96,0},{112,16},{1... | collective-permute-start | bytes 589832 | tf_op jit(solution)/shard_map/ppermute | solution.py:241
  85.7 13.1 %collective-permute-start.6 = (bf16[384,256]{1,0:T(8,128)(2,1)}, bf16[384,256]{1,0:T(8,128)(2,1)S(1)}, u32[]{:S(2)}, u32[]{:S(2)}) collective-permute-start(bf16[384,256]{1,0:T(8,128)(2,1)} %add.2.refs_0_), channel_id=1, source_target_pairs={{0,16},{16,0},{32,48},{48,32},{64,80},{80,64},{96,112},{112,96},{1... | collective-permute-start | bytes 589832 | tf_op jit(solution)/shard_map/ppermute | solution.py:243
  91.0 8.9 %copy-start.2 = (bf16[384,256]{1,0:T(8,128)(2,1)}, bf16[384,256]{1,0:T(8,128)(2,1)S(1)}, u32[]{:S(2)}) copy-start(bf16[384,256]{1,0:T(8,128)(2,1)S(1)} %collective-permute-done.5.refs_3_) | copy-start | bytes 589828
  91.0 7.8 %collective-permute-start.9 = (bf16[384,256]{1,0:T(8,128)(2,1)S(1)}, bf16[384,256]{1,0:T(8,128)(2,1)S(1)}, u32[]{:S(2)}, u32[]{:S(2)}) collective-permute-start(bf16[384,256]{1,0:T(8,128)(2,1)S(1)} %collective-permute-done.5.refs_3_), channel_id=1, source_target_pairs={{0,16},{16,0},{32,48},{48,32},{64,80},{80,64},{96,112},{112,96},{1... | collective-permute-start | bytes 589832 | tf_op jit(solution)/shard_map/ppermute | solution.py:243
  94.4 5.5 %copy-start.3 = (bf16[384,256]{1,0:T(8,128)(2,1)}, bf16[384,256]{1,0:T(8,128)(2,1)S(1)}, u32[]{:S(2)}) copy-start(bf16[384,256]{1,0:T(8,128)(2,1)S(1)} %collective-permute-done.4.refs_2_) | copy-start | bytes 589828
  94.4 4.4 %collective-permute-start.8 = (bf16[384,256]{1,0:T(8,128)(2,1)S(1)}, bf16[384,256]{1,0:T(8,128)(2,1)S(1)}, u32[]{:S(2)}, u32[]{:S(2)}) collective-permute-start(bf16[384,256]{1,0:T(8,128)(2,1)S(1)} %collective-permute-done.4.refs_2_), channel_id=1, source_target_pairs={{0,16},{16,0},{32,48},{48,32},{64,80},{80,64},{96,112},{112,96},{1... | collective-permute-start | bytes 589832 | tf_op jit(solution)/shard_map/ppermute | solution.py:243
  96.8 3.1 %copy-start.4 = (bf16[384,256]{1,0:T(8,128)(2,1)}, bf16[384,256]{1,0:T(8,128)(2,1)S(1)}, u32[]{:S(2)}) copy-start(bf16[384,256]{1,0:T(8,128)(2,1)S(1)} %collective-permute-done.3.refs_1_) | copy-start | bytes 589828
  96.8 3.1 %collective-permute-start.7 = (bf16[384,256]{1,0:T(8,128)(2,1)S(1)}, bf16[384,256]{1,0:T(8,128)(2,1)S(1)}, u32[]{:S(2)}, u32[]{:S(2)}) collective-permute-start(bf16[384,256]{1,0:T(8,128)(2,1)S(1)} %collective-permute-done.3.refs_1_), channel_id=1, source_target_pairs={{0,16},{16,0},{32,48},{48,32},{64,80},{80,64},{96,112},{112,96},{1... | collective-permute-start | bytes 589832 | tf_op jit(solution)/shard_map/ppermute | solution.py:243
  98.8 1.1 %copy-start.5 = (bf16[384,256]{1,0:T(8,128)(2,1)}, bf16[384,256]{1,0:T(8,128)(2,1)S(1)}, u32[]{:S(2)}) copy-start(bf16[384,256]{1,0:T(8,128)(2,1)S(1)} %collective-permute-done.6.refs_4_) | copy-start | bytes 589828
  98.8 1.1 %copy-start.6 = (bf16[384,256]{1,0:T(8,128)(2,1)}, bf16[384,256]{1,0:T(8,128)(2,1)S(1)}, u32[]{:S(2)}) copy-start(bf16[384,256]{1,0:T(8,128)(2,1)S(1)} %collective-permute-done.9.refs_7_) | copy-start | bytes 589828
  98.8 1.1 %copy-start.7 = (bf16[384,256]{1,0:T(8,128)(2,1)}, bf16[384,256]{1,0:T(8,128)(2,1)S(1)}, u32[]{:S(2)}) copy-start(bf16[384,256]{1,0:T(8,128)(2,1)S(1)} %collective-permute-done.8.refs_6_) | copy-start | bytes 589828
  99.9 0.7 copy-start.8

commit v2 on v1

--- a/solution.py
+++ b/solution.py
@@ -16,6 +16,11 @@
 
 VMEM = pl.BlockSpec(memory_space=pltpu.VMEM)
 SMEM = pl.BlockSpec(memory_space=pltpu.SMEM)
+ANY = pl.BlockSpec(memory_space=pl.ANY)
+
+
+def in_vmem(array):
+    return pltpu.with_memory_space_constraint(array, pltpu.VMEM)
 
 
 def request_kernel(owners, blk_dev, coords, count, wanted, slots, used):
@@ -41,48 +46,63 @@
         wanted[owner] = jnp.broadcast_to(table[owner : owner + 1], wanted.shape[1:])
 
 
-def serve_kernel(peers, asked, factors, sent, table):
+def serve_kernel(peers, asked, factors, tiles, sent, table, first, listed, held, ready, sems):
+    copy = pltpu.make_async_copy(asked.at[:, 0, :], listed, sems.at[0])
+    copy.start()
+    whole = pltpu.make_async_copy(factors, held, sems.at[6])
+    whole.start()
+    early = pltpu.make_async_copy(tiles.at[0], first, sems.at[1])
+    early.start()
+    copy.wait()
     lane = lax.broadcasted_iota(jnp.int32, table.shape, 1)
-    listed = jnp.full(table.shape, -1, jnp.int32)
+    line = jnp.full(table.shape, -1, jnp.int32)
     for peer in range(peers):
         for rank in range(CAP):
-            local = asked[peer, 0, rank]
-            listed = jnp.where(lane == peer * CAP + rank, local, listed)
-            sent[peer, rank * TILE : (rank + 1) * TILE, :] = factors[jnp.maximum(local, 0)].astype(
-                jnp.bfloat16
+            line = jnp.where(lane == peer * CAP + rank, listed[peer, rank], line)
+    table[...] = line
+    whole.wait()
+    group = peers // 4
+    copies = []
+    for peer in range(peers):
+        for rank in range(CAP):
+            local = jnp.maximum(listed[peer, rank], 0)
+            ready[peer, rank * TILE : (rank + 1) * TILE, :] = held[local].astype(jnp.bfloat16)
+        if peer % group == group - 1:
+            some = slice(peer + 1 - group, peer + 1)
+            copies.append(
+                pltpu.make_async_copy(ready.at[some], sent.at[some], sems.at[2 + peer // group])
             )
-    table[...] = listed
+            copies[-1].start()
+    for copy in copies:
+        copy.wait()
+    early.wait()
 
 
 def tile_kernel(
-    owners, parts, chunk, count, slots, blocks, tiles, out, values, misfit, pair_ab, pair_cd, grads, sem
+    owners, parts, chunk, count, slots, blocks, early, tiles, out, values, misfit, pair_ab, pair_cd, grads, sems
 ):
-    live = count[0]
+    live, total = count[0], tiles.shape[0]
     f32, bf16 = jnp.float32, jnp.bfloat16
     rank = blocks.shape[-1]
+    spare = owners * CAP
 
     def fetch(slot):
-        place = lax.rem(slot, 2)
-        return pltpu.make_async_copy(tiles.at[slot], values.at[place], sem.at[place])
-
-    fetch(0).start()
+        return pltpu.make_async_copy(tiles.at[slot], values.at[slot], sems.at[slot])
+
+    for slot in range(1, total):
+        fetch(slot).start()
     grads[...] = jnp.zeros_like(grads)
 
-    def tile(slot, carry):
-        @pl.when(slot + 1 < live)
-        def _():
-            fetch(slot + 1).start()
-
-        names = [slots[slot * 4 + mode] for mode in range(4)]
+    def tile(slot, tile_at):
+        names = [jnp.where(slot < live, slots[slot * 4 + mode], spare) for mode in range(4)]
         one, two, three, four = [
-            blocks[pl.ds(pl.multiple_of(name * TILE, TILE), TILE), :].astype(f32) for name in names
+            blocks[pl.ds(pl.multiple_of(jnp.minimum(name, spare - 1) * TILE, TILE), TILE), :].astype(f32)
+            for name in names
         ]
         for i in range(TILE):
             at = slice(i * TILE, (i + 1) * TILE)
             pair_ab[at, :] = (one[i : i + 1] * two).astype(bf16)
             pair_cd[at, :] = (three[i : i + 1] * four).astype(bf16)
-        fetch(slot).wait()
-        place = lax.rem(slot, 2)
         outer = chunk // TILE
         grad_one, grad_two = [], jnp.zeros((TILE, rank), f32)
         for at in range(0, EDGE, chunk):
@@ -92,7 +112,8 @@
                 (((1,), (1,)), ((), ())),
                 preferred_element_type=f32,
             )
-            off = jnp.clip(model - values[place, at : at + chunk, :].astype(f32), -1.0, 1.0).astype(bf16)
+            off = (model - tile_at[at : at + chunk, :].astype(f32)).astype(bf16)
+            off = jnp.clip(off, jnp.asarray(-1.0, bf16), jnp.asarray(1.0, bf16))
             misfit[at : at + chunk, :] = off
             left = jnp.dot(off, pair_cd[...], preferred_element_type=f32).reshape(outer, TILE, rank)
             grad_one.append(jnp.sum(left * two[None], axis=1))
@@ -115,9 +136,14 @@
         grads[names[1]] = grad_two
         grads[names[2]] = jnp.concatenate(grad_three, 0)
         grads[names[3]] = grad_four
+
+    def later(slot, carry):
+        fetch(slot).wait()
+        tile(slot, values.at[slot])
         return carry
 
-    lax.fori_loop(0, live, tile, 0)
+    tile(0, early)
+    lax.fori_loop(1, total, later, 0)
     height = TILE // parts
     for owner in range(owners):
         for part in range(parts):
@@ -151,15 +177,33 @@
 
 
 def update_kernel(layer, factors, *refs):
-    own, other, out = refs[:4], refs[4:8], refs[8]
+    own, other, (out, before, stepped, sems) = refs[:4], refs[4:8], refs[8:]
     parts = len(own)
     height = TILE // parts
-    for back in range(parts):
-        source = lax.rem(layer[0] + parts - back, parts)
-        at = pl.ds(pl.multiple_of(source * height, height), height)
-        gradient = own[back][...].astype(jnp.float32) + other[back][...].astype(jnp.float32)
-        gradient = gradient.reshape(out.shape[0], height, -1)
-        out[:, at, :] = factors[:, at, :] - step_size * gradient
+    held = factors.shape[0] // 4
+    modes = [slice(mode * held, (mode + 1) * held) for mode in range(4)]
+    brought = [
+        pltpu.make_async_copy(factors.at[blocks], before.at[blocks], sems.at[mode])
+        for mode, blocks in enumerate(modes)
+    ]
+    stored = [
+        pltpu.make_async_copy(stepped.at[blocks], out.at[blocks], sems.at[4 + mode])
+        for mode, blocks in enumerate(modes)
+    ]
+    for copy in brought:
+        copy.start()
+    for mode, blocks in enumerate(modes):
+        brought[mode].wait()
+        lines = slice(mode * held * height, (mode + 1) * held * height)
+        for back in range(parts):
+            source = lax.rem(layer[0] + parts - back, parts)
+            at = pl.ds(pl.multiple_of(source * height, height), height)
+            gradient = own[back][lines, :].astype(jnp.float32) + other[back][lines, :].astype(jnp.float32)
+            gradient = gradient.reshape(held, height, -1)
+            stepped[blocks, at, :] = before[blocks, at, :] - step_size * gradient
+        stored[mode].start()
+    for copy in stored:
+        copy.wait()
 
 
 def on_device(layers, owners, tile_values, tile_coords, tile_count, factors):
@@ -174,7 +218,7 @@
     wanted, slots = pl.pallas_call(
         functools.partial(request_kernel, owners, blk_dev),
         out_shape=(
-            jax.ShapeDtypeStruct((owners, 8, LANES), i32),
+            pltpu.VMEM((owners, 8, LANES), i32),
             jax.ShapeDtypeStruct((slot_total * 4,), i32),
         ),
         in_specs=[SMEM, SMEM],
@@ -184,16 +228,23 @@
     )(tile_coords[0].T, tile_count)
     asked = lax.all_to_all(wanted, "rows", 0, 0)
 
-    sent, table = pl.pallas_call(
+    sent, table, first = pl.pallas_call(
         functools.partial(serve_kernel, owners),
         out_shape=(
             jax.ShapeDtypeStruct((owners, CAP * TILE, rank), bf16),
             jax.ShapeDtypeStruct((8, LANES), i32),
+            pltpu.VMEM(tile_values.shape[2:], bf16),
         ),
-        in_specs=[SMEM, VMEM],
-        out_specs=(VMEM, VMEM),
+        in_specs=[ANY, ANY, ANY],
+        out_specs=(ANY, VMEM, VMEM),
+        scratch_shapes=[
+            pltpu.SMEM((owners, LANES), i32),
+            pltpu.VMEM(factor_blocks.shape, f32),
+            pltpu.VMEM((owners, CAP * TILE, rank), bf16),
+            pltpu.SemaphoreType.DMA((7,)),
+        ],
         name="serve",
-    )(asked, factor_blocks)
+    )(in_vmem(asked), factor_blocks, tile_values[0])
     blocks = lax.all_to_all(sent, "rows", 0, 0).reshape(owners * CAP * TILE, rank)
 
     def round_trip(back):
@@ -202,26 +253,27 @@
 
     tables = [table] + [lax.ppermute(table, "tiles", round_trip(back)) for back in range(1, layers)]
 
+    slots, tables, layer = lax.optimization_barrier((slots, tables, layer))
     flops = 3 * 2 * EDGE * EDGE * rank * slot_total
     messages = pl.pallas_call(
         functools.partial(tile_kernel, owners, layers, 256),
-        out_shape=jax.ShapeDtypeStruct((layers * owners, CAP * TILE // layers, rank), bf16),
-        in_specs=[SMEM, SMEM, VMEM, pl.BlockSpec(memory_space=pl.ANY)],
+        out_shape=pltpu.VMEM((layers * owners, CAP * TILE // layers, rank), bf16),
+        in_specs=[SMEM, SMEM, VMEM, VMEM, ANY],
         out_specs=VMEM,
         scratch_shapes=[
-            pltpu.VMEM((2, EDGE, EDGE), bf16),
+            pltpu.VMEM((slot_total, EDGE, EDGE), bf16),
             pltpu.VMEM((EDGE, EDGE), bf16),
             pltpu.VMEM((EDGE, rank), bf16),
             pltpu.VMEM((EDGE, rank), bf16),
-            pltpu.VMEM((owners * CAP, TILE, rank), f32),
-            pltpu.SemaphoreType.DMA((2,)),
+            pltpu.VMEM((owners * CAP + 1, TILE, rank), f32),
+            pltpu.SemaphoreType.DMA((slot_total,)),
         ],
         compiler_params=pltpu.CompilerParams(vmem_limit_bytes=40 << 20),
         cost_estimate=pl.CostEstimate(
             flops=flops, bytes_accessed=2 * EDGE * EDGE * slot_total, transcendentals=0
         ),
         name="tiles",
-    )(tile_count, slots, blocks, tile_values[0])
+    )(tile_count, slots, in_vmem(blocks), in_vmem(first), tile_values[0])
 
     same_core = [
         [t * owners + r for t in range(core, 2 * layers, 2) for r in range(owners)] for core in range(2)
@@ -231,12 +283,12 @@
     height = TILE // layers
     partial = pl.pallas_call(
         functools.partial(add_kernel, owners),
-        out_shape=jax.ShapeDtypeStruct((held * height, rank), bf16),
+        out_shape=pltpu.VMEM((held * height, rank), bf16),
         in_specs=[SMEM] * (1 + layers) + [VMEM],
         out_specs=VMEM,
         scratch_shapes=[pltpu.VMEM((held, height, rank), f32)] * CAP,
         name="add",
-    )(layer, *tables, came)
+    )(layer, *tables, in_vmem(came))
 
     own = [partial] + [lax.ppermute(partial, "tiles", round_trip(back)) for back in range(1, layers)]
     pair = [(i, i ^ 1) for i in range(2 * layers)]
@@ -245,10 +297,11 @@
     updated = pl.pallas_call(
         update_kernel,
         out_shape=jax.ShapeDtypeStruct(factor_blocks.shape, f32),
-        in_specs=[SMEM] + [VMEM] * 9,
-        out_specs=VMEM,
+        in_specs=[SMEM, ANY] + [VMEM] * 8,
+        out_specs=ANY,
+        scratch_shapes=[pltpu.VMEM(factor_blocks.shape, f32)] * 2 + [pltpu.SemaphoreType.DMA((8,))],
         name="update",
-    )(layer, factor_blocks, *own, *other)
+    )(layer, factor_blocks, *[in_vmem(piece) for piece in own + other])
     return updated.reshape(factors.shape)
 
 

time: 104 us -> 99.5 us (0.957)
  starting transfers between devices: 28.9 us -> 22 us
  blocking collectives: 33.3 us -> 38.5 us
  local copies, waits for them, and re-layouts: 1.67 us -> 0.02 us
  waiting for transfers between devices: 13 us -> 11.8 us
    all_to_all x1, starting transfers between devices: 10.8 us -> 3.67 us  [on_device(): lax.all_to_all(sent, 'rows', 0, 0).reshape(owners * CAP * TILE, rank)]
    all_to_all x1, blocking collectives: 19.1 us -> 24.5 us  [on_device(): lax.all_to_all(messages, ('tiles', 'rows'), 0, 0, axis_index_groups=same_...]
    unnamed x26 -> x10, local copies, waits for them, and re-layouts: 1.67 us -> 0.02 us
    ppermute x4, starting transfers between devices: 13.1 us -> 11.7 us  [on_device(): other = [lax.ppermute(piece, 'tiles', pair) for piece in own]]
    pallas_call x1, Pallas kernels: 15.9 us -> 17.2 us  [on_device(): pl.pallas_call(functools.partial(tile_kernel, owners, layers, 256), out_s...]
    all_to_all x1, waiting for transfers between devices: 8.63 us -> 7.44 us  [on_device(): lax.all_to_all(sent, 'rows', 0, 0).reshape(owners * CAP * TILE, rank)]
    pallas_call x1, Pallas kernels: 3.35 us -> 2.27 us  [on_device(): pl.pallas_call(update_kernel, out_shape=jax.ShapeDtypeStruct(factor_block...]
where the time goes in v2:
time: 99.5 us; the launch traced here: 98.6 us
  blocking collectives  38.5 us (39%)
  Pallas kernels  25.6 us (26%)
  starting transfers between devices  22 us (22%)
  waiting for transfers between devices  11.8 us (12%)
    all_to_all x1, blocking collectives, on_device(): lax.all_to_all(messages, ('tiles', 'rows'), 0, 0, axis_index_groups=same_...  24.5 us
    pallas_call x1, Pallas kernels, on_device(): pl.pallas_call(functools.partial(tile_kernel, owners, layers, 256), out_s...  17.2 us
    all_to_all x1, blocking collectives, on_device(): asked = lax.all_to_all(wanted, 'rows', 0, 0)  14 us
    ppermute x4, starting transfers between devices, on_device(): other = [lax.ppermute(piece, 'tiles', pair) for piece in own]  11.7 us
    all_to_all x1, waiting for transfers between devices, on_device(): lax.all_to_all(sent, 'rows', 0, 0).reshape(owners * CAP * TILE, rank)  7.44 us
    ppermute x3, starting transfers between devices, on_device(): lax.ppermute(table, 'tiles', round_trip(back))  4.33 us
    all_to_all x1, starting transfers between devices, on_device(): lax.all_to_all(sent, 'rows', 0, 0).reshape(owners * CAP * TILE, rank)  3.67 us
    ppermute x3, waiting for transfers between devices, on_device(): lax.ppermute(table, 'tiles', round_trip(back))  3.26 us
  transfers between devices with their start and end apart: 11, of which 4 were waited for; matrix products, arithmetic and copies ran while one was open for 0% of the time, Pallas kernels for 0%

profile of v2, /device:TPU:1, one launch (start us, length us, event | category | flops | bytes accessed | tf_op | source)
XLA Modules:
  0.0 98.6 jit_solution(13170117117716963855)
XLA Ops:
  0.7 1.5 %requests.1 = (s32[16,8,128]{2,1,0:T(8,128)S(1)}, s32[32]{0:T(128)}) custom-call(s32[4,8]{1,0:T(4,128)} %bitcast.13, s32[1]{0:T(128)S(6)} %copy.5.count), custom_call_target="tpu_custom_call" | custom-call | tf_op jit(solution)/shard_map/requests/pallas_call | solution.py:218
  2.2 14.0 %all_to_all.15.asked = s32[16,8,128]{2,1,0:T(8,128)S(1)} all-to-all(s32[16,8,128]{2,1,0:T(8,128)S(1)} %get-tuple-element.17), channel_id=1, replica_groups=mesh['tiles'=8,'rows'=16] {'rows'}, dimensions={0} | all-to-all | bytes 131072 | tf_op jit(solution)/shard_map/all_to_all | solution.py:229
  16.1 3.0 %serve.1 = (bf16[16,128,256]{2,1,0:T(8,128)(2,1)}, s32[8,128]{1,0:T(8,128)}, bf16[1024,1024]{1,0:T(8,128)(2,1)S(1)}) custom-call(s32[16,8,128]{2,1,0:T(8,128)S(1)} %all_to_all.15.asked, f32[48,32,256]{2,1,0:T(8,128)} %bitcast.11, bf16[8,1024,1024]{2,1,0:T(8,128)(2,1)} %bitcast.9), custom_call_target="tpu_custom_call" | custom-call | tf_op jit(solution)/shard_map/serve/pallas_call | solution.py:231
  19.2 0.0 copy-start.1
  19.2 0.0 copy-start
  19.2 3.7 %all-to-all-start.1 = ((bf16[16,128,256]{2,1,0:T(8,128)(2,1)}), bf16[16,128,256]{2,1,0:T(8,128)(2,1)S(1)}, u32[]{:S(2)}, u32[]{:S(2)}) async-start(bf16[16,128,256]{2,1,0:T(8,128)(2,1)} %get-tuple-element.25), calls=%async_computation.1 | async-start | bytes 2097152 | tf_op jit(solution)/shard_map/all_to_all | solution.py:248
  22.9 0.0 copy-done.1
  22.9 3.6 %collective-permute-start.2 = (s32[8,128]{1,0:T(8,128)S(1)}, s32[8,128]{1,0:T(8,128)S(1)}, u32[]{:S(2)}, u32[]{:S(2)}) collective-permute-start(s32[8,128]{1,0:T(8,128)S(1)} %copy-done.1), channel_id=1, source_target_pairs={{0,96},{16,112},{32,0},{48,16},{64,32},{80,48},{96,64},{112,80},{1... | collective-permute-start | bytes 12296 | tf_op jit(solution)/shard_map/ppermute | solution.py:254
  26.5 0.0 collective-permute-start.1
  26.5 0.7 collective-permute-start
  27.2 0.1 collective-permute-done.2.table_3
  27.3 3.2 %collective-permute-done.1.table_2 = s32[8,128]{1,0:T(8,128)S(1)} collective-permute-done((s32[8,128]{1,0:T(8,128)S(1)}, s32[8,128]{1,0:T(8,128)S(1)}, u32[]{:S(2)}, u32[]{:S(2)}) %collective-permute-start.1) | collective-permute-done | bytes 4128 | tf_op jit(solution)/shard_map/ppermute | solution.py:254
  30.5 0.0 collective-permute-done.table_1
  30.5 7.4 %all-to-all-done.1 = bf16[16,128,256]{2,1,0:T(8,128)(2,1)S(1)} async-done(((bf16[16,128,256]{2,1,0:T(8,128)(2,1)}), bf16[16,128,256]{2,1,0:T(8,128)(2,1)S(1)}, u32[]{:S(2)}, u32[]{:S(2)}) %all-to-all-start.1) | async-done | bytes 1048608 | tf_op jit(solution)/shard_map/all_to_all | solution.py:248
  37.9 17.2 %tiles.1 = bf16[64,32,256]{2,1,0:T(8,128)(2,1)S(1)} custom-call(s32[1]{0:T(128)S(6)} %copy.5.count, s32[32]{0:T(128)S(1)} %copy-done, bf16[2048,256]{1,0:T(8,128)(2,1)S(1)} %bitcast.8, bf16[1024,1024]{1,0:T(8,128)(2,1)S(1)} %get-tuple-element.26.early, bf16[8,1024,1024]{2,1,0:T(8,128)(2,1)} %bitcast.10), custom_call_target="tpu_custom_call" | custom-call | flops 12884901888 | bytes 16777216 | tf_op jit(solution)/shard_map/tiles/pallas_call | solution.py:258
  55.1 24.5 %all_to_all.16.came = bf16[64,32,256]{2,1,0:T(8,128)(2,1)S(1)} all-to-all(bf16[64,32,256]{2,1,0:T(8,128)(2,1)S(1)} %tiles.1), channel_id=1, replica_groups={{0,1,2,3,4,5,6,7,8,9,10,11,12,13,14,15,32,33,34,35,36,37,38,39,40,41,42..., dimensions={0} | all-to-all | bytes 2097152 | tf_op jit(solution)/shard_map/all_to_all | solution.py:281
  79.6 1.6 %add.2.refs_0_ = bf16[384,256]{1,0:T(8,128)(2,1)S(1)} custom-call(s32[1]{0:T(128)} %bitcast.4.layer, s32[8,128]{1,0:T(8,128)} %get-tuple-element.20.table_0, s32[8,128]{1,0:T(8,128)} %copy-done.4, s32[8,128]{1,0:T(8,128)} %copy-done.3, s32[8,128]{1,0:T(8,128)} %copy-done.2, bf16[64,32,256]{2,1,0:T(8,128)(2,1)S(1)} %all_to_all.16.came), custom_call_target="tpu_custom_call" | custom-call | tf_op jit(solution)/shard_map/add/pallas_call | solution.py:284
  81.2 1.0 collective-permute-start.5
  82.2 1.3 %collective-permute-start.4 = (bf16[384,256]{1,0:T(8,128)(2,1)S(1)}, bf16[384,256]{1,0:T(8,128)(2,1)S(1)}, u32[]{:S(2)}, u32[]{:S(2)}) collective-permute-start(bf16[384,256]{1,0:T(8,128)(2,1)S(1)} %add.2.refs_0_), channel_id=1, source_target_pairs={{0,64},{16,80},{32,96},{48,112},{64,0},{80,16},{96,32},{112,48},{1... | collective-permute-start | bytes 589832 | tf_op jit(solution)/shard_map/ppermute | solution.py:293
  83.5 0.0 collective-permute-start.3
  83.5 3.9 %collective-permute-start.6 = (bf16[384,256]{1,0:T(8,128)(2,1)S(1)}, bf16[384,256]{1,0:T(8,128)(2,1)S(1)}, u32[]{:S(2)}, u32[]{:S(2)}) collective-permute-start(bf16[384,256]{1,0:T(8,128)(2,1)S(1)} %add.2.refs_0_), channel_id=1, source_target_pairs={{0,16},{16,0},{32,48},{48,32},{64,80},{80,64},{96,112},{112,96},{1... | collective-permute-start | bytes 589832 | tf_op jit(solution)/shard_map/ppermute | solution.py:295
  87.3 0.0 collective-permute-done.5.refs_3_
  87.4 3.4 %collective-permute-start.9 = (bf16[384,256]{1,0:T(8,128)(2,1)S(1)}, bf16[384,256]{1,0:T(8,128)(2,1)S(1)}, u32[]{:S(2)}, u32[]{:S(2)}) collective-permute-start(bf16[384,256]{1,0:T(8,128)(2,1)S(1)} %collective-permute-done.5.refs_3_), channel_id=1, source_target_pairs={{0,16},{16,0},{32,48},{48,32},{64,80},{80,64},{96,112},{112,96},{1... | collective-permute-start | bytes 589832 | tf_op jit(solution)/shard_map/ppermute | solution.py:295
  90.7 0.0 collective-permute-done.4.refs_2_
  90.7 2.5 %collective-permute-start.8 = (bf16[384,256]{1,0:T(8,128)(2,1)S(1)}, bf16[384,256]{1,0:T(8,128)(2,1)S(1)}, u32[]{:S(2)}, u32[]{:S(2)}) collective-permute-start(bf16[384,256]{1,0:T(8,128)(2,1)S(1)} %collective-permute-done.4.refs_2_), channel_id=1, source_target_pairs={{0,16},{16,0},{32,48},{48,32},{64,80},{80,64},{96,112},{112,96},{1... | collective-permute-start | bytes 589832 | tf_op jit(solution)/shard_map/ppermute | solution.py:295
  93.2 0.0 collective-permute-done.3.refs_1_
  93.2 2.0 %collective-permute-start.7 = (bf16[384,256]{1,0:T(8,128)(2,1)S(1)}, bf16[384,256]{1,0:T(8,128)(2,1)S(1)}, u32[]{:S(2)}, u32[]{:S(2)}) collective-permute-start(bf16[384,256]{1,0:T(8,128)(2,1)S(1)} %collective-permute-done.3.refs_1_), channel_id=1, source_target_pairs={{0,16},{16,0},{32,48},{48,32},{64,80},{80,64},{96,112},{112,96},{1... | collective-permute-start | bytes 589832 | tf_op jit(solution)/shard_map/ppermute | solution.py:295
  95.2 0.0 collective-permute-done.6.refs_4_
  95.2 0.0 collective-permute-done.9.refs_7_
  95.2 0.0 collective-permute-done.8.refs_6_
  95.3 1.1 %collective-permute-done.7.refs_5_ = bf16[384,256]{1,0:T(8,128)(2,1)S(1)} collective-permute-done((bf16[384,256]{1,0:T(8,128)(2,1)S(1)}, bf16[384,256]{1,0:T(8,128)(2,1)S(1)}, u32[]{:S(2)}, u32[]{:S(2)}) %collective-permute-start.7) | collective-permute-done | bytes 196640 | tf_op jit(solution)/shard_map/ppermute | solution.py:295
  96.3 2.3 %update.1 = f32[48,32,256]{2,1,0:T(8,128)} custom-call(s32[1]{0:T(128)} %bitcast.4.layer, f32[48,32,256]{2,1,0:T(8,128)} %bitcast.12, bf16[384,256]{1,0:T(8,128)(2,1)S(1)} %add.2.refs_0_, bf16[384,256]{1,0:T(8,128)(2,1)S(1)} %collective-permute-done.3.refs_1_, bf16[384,256]{1,0:T(8,128)(2,1)S(1)} %collective-permute-done.4.refs_2_, ...), custom_call_target="tpu_custom_call" | custom-call | tf_op jit(solution)/shard_map/update/pallas_call | solution.py:297
  (7 shorter events, 0.0 us)
Async XLA Ops:
  19.2 3.7 %copy-start.1 = (s32[8,128]{1,0:T(8,128)S(1)}, s32[8,128]{1,0:T(8,128)}, u32[]{:S(2)}) copy-start(s32[8,128]{1,0:T(8,128)} %get-tuple-element.20.table_0) | copy-start | bytes 12292
  19.2 18.7 %copy-start = (s32[32]{0:T(128)S(1)}, s32[32]{0:T(128)}, u32[]{:S(2)}) copy-start(s32[32]{0:T(128)} %get-tuple-element.24.slots) | copy-start | bytes 388
  19.2 18.7 %all-to-all-start.1 = ((bf16[16,128,256]{2,1,0:T(8,128)(2,1)}), bf16[16,128,256]{2,1,0:T(8,128)(2,1)S(1)}, u32[]{:S(2)}, u32[]{:S(2)}) async-start(bf16[16,128,256]{2,1,0:T(8,128)(2,1)} %get-tuple-element.25), calls=%async_computation.1 | async-start | bytes 2097152 | tf_op jit(solution)/shard_map/all_to_all | solution.py:248
  22.9 4.4 %collective-permute-start.2 = (s32[8,128]{1,0:T(8,128)S(1)}, s32[8,128]{1,0:T(8,128)S(1)}, u32[]{:S(2)}, u32[]{:S(2)}) collective-permute-start(s32[8,128]{1,0:T(8,128)S(1)} %copy-done.1), channel_id=1, source_target_pairs={{0,96},{16,112},{32,0},{48,16},{64,32},{80,48},{96,64},{112,80},{1... | collective-permute-start | bytes 12296 | tf_op jit(solution)/shard_map/ppermute | solution.py:254
  26.5 4.0 %collective-permute-start.1 = (s32[8,128]{1,0:T(8,128)S(1)}, s32[8,128]{1,0:T(8,128)S(1)}, u32[]{:S(2)}, u32[]{:S(2)}) collective-permute-start(s32[8,128]{1,0:T(8,128)S(1)} %copy-done.1), channel_id=1, source_target_pairs={{0,64},{16,80},{32,96},{48,112},{64,0},{80,16},{96,32},{112,48},{1... | collective-permute-start | bytes 12296 | tf_op jit(solution)/shard_map/ppermute | solution.py:254
  26.5 4.0 %collective-permute-start = (s32[8,128]{1,0:T(8,128)S(1)}, s32[8,128]{1,0:T(8,128)S(1)}, u32[]{:S(2)}, u32[]{:S(2)}) collective-permute-start(s32[8,128]{1,0:T(8,128)S(1)} %copy-done.1), channel_id=1, source_target_pairs={{0,32},{16,48},{32,64},{48,80},{64,96},{80,112},{96,0},{112,16},{1... | collective-permute-start | bytes 12296 | tf_op jit(solution)/shard_map/ppermute | solution.py:254
  27.3 27.8 %copy-start.2 = (s32[8,128]{1,0:T(8,128)}, s32[8,128]{1,0:T(8,128)S(1)}, u32[]{:S(2)}) copy-start(s32[8,128]{1,0:T(8,128)S(1)} %collective-permute-done.2.table_3) | copy-start | bytes 12292
  30.5 24.6 %copy-start.3 = (s32[8,128]{1,0:T(8,128)}, s32[8,128]{1,0:T(8,128)S(1)}, u32[]{:S(2)}) copy-start(s32[8,128]{1,0:T(8,128)S(1)} %collective-permute-done.1.table_2) | copy-start | bytes 12292
  30.5 24.6 %copy-start.4 = (s32[8,128]{1,0:T(8,128)}, s32[8,128]{1,0:T(8,128)S(1)}, u32[]{:S(2)}) copy-start(s32[8,128]{1,0:T(8,128)S(1)} %collective-permute-done.table_1) | copy-start | bytes 12292
  81.2 6.1 %collective-permute-start.5 = (bf16[384,256]{1,0:T(8,128)(2,1)S(1)}, bf16[384,256]{1,0:T(8,128)(2,1)S(1)}, u32[]{:S(2)}, u32[]{:S(2)}) collective-permute-start(bf16[384,256]{1,0:T(8,128)(2,1)S(1)} %add.2.refs_0_), channel_id=1, source_target_pairs={{0,96},{16,112},{32,0},{48,16},{64,32},{80,48},{96,64},{112,80},{1... | collective-permute-start | bytes 589832 | tf_op jit(solution)/shard_map/ppermute | solution.py:293
  82.2 8.5 %collective-permute-start.4 = (bf16[384,256]{1,0:T(8,128)(2,1)S(1)}, bf16[384,256]{1,0:T(8,128)(2,1)S(1)}, u32[]{:S(2)}, u32[]{:S(2)}) collective-permute-start(bf16[384,256]{1,0:T(8,128)(2,1)S(1)} %add.2.refs_0_), channel_id=1, source_target_pairs={{0,64},{16,80},{32,96},{48,112},{64,0},{80,16},{96,32},{112,48},{1... | collective-permute-start | bytes 589832 | tf_op jit(solution)/shard_map/ppermute | solution.py:293
  83.5 9.8 %collective-permute-start.3 = (bf16[384,256]{1,0:T(8,128)(2,1)S(1)}, bf16[384,256]{1,0:T(8,128)(2,1)S(1)}, u32[]{:S(2)}, u32[]{:S(2)}) collective-permute-start(bf16[384,256]{1,0:T(8,128)(2,1)S(1)} %add.2.refs_0_), channel_id=1, source_target_pairs={{0,32},{16,48},{32,64},{48,80},{64,96},{80,112},{96,0},{112,16},{1... | collective-permute-start | bytes 589832 | tf_op jit(solution)/shard_map/ppermute | solution.py:293
  83.5 11.8 %collective-permute-start.6 = (bf16[384,256]{1,0:T(8,128)(2,1)S(1)}, bf16[384,256]{1,0:T(8,128)(2,1)S(1)}, u32[]{:S(2)}, u32[]{:S(2)}) collective-permute-start(bf16[384,256]{1,0:T(8,128)(2,1)S(1)} %add.2.refs_0_), channel_id=1, source_target_pairs={{0,16},{16,0},{32,48},{48,32},{64,80},{80,64},{96,112},{112,96},{1... | collective-permute-start | bytes 589832 | tf_op jit(solution)/shard_map/ppermute | solution.py:295
  87.4 7.9 %collective-permute-start.9 = (bf16[384,256]{1,0:T(8,128)(2,1)S(1)}, bf16[384,256]{1,0:T(8,128)(2,1)S(1)}, u32[]{:S(2)}, u32[]{:S(2)}) collective-permute-start(bf16[384,256]{1,0:T(8,128)(2,1)S(1)} %collective-permute-done.5.refs_3_), channel_id=1, source_target_pairs={{0,16},{16,0},{32,48},{48,32},{64,80},{80,64},{96,112},{112,96},{1... | collective-permute-start | bytes 589832 | tf_op jit(solution)/shard_map/ppermute | solution.py:295
  90.7 4.5 %collective-permute-start.8 = (bf16[384,256]{1,0:T(8,128)(2,1)S(1)}, bf16[384,256]{1,0:T(8,128)(2,1)S(1)}, u32[]{:S(2)}, u32[]{:S(2)}) collective-permute-start(bf16[384,256]{1,0:T(8,128)(2,1)S(1)} %collective-permute-done.4.refs_2_), channel_id=1, source_target_pairs={{0,16},{16,0},{32,48},{48,32},{64,80},{80,64},{96,112},{112,96},{1... | collective-permute-start | bytes 589832 | tf_op jit(solution)/shard_map/ppermute | solution.py:295
  93.2 3.1 %collective-permute-start.7 = (bf16[384,256]{1,0:T(8,128)(2,1)S(1)}, bf16[384,256]{1,0:T(8,128)(2,1)S(1)}, u32[]{:S(2)}, u32[]{:S(2)}) collective-permute-start(bf16[384,256]{1,0:T(8,128)(2,1)S(1)} %collective-permute-done.3.refs_1_), channel_id=1, source_target_pairs={{0,16},{16,0},{32,48},{48,32},{64,80},{80,64},{96,112},{112,96},{1... | collective-permute-start | bytes 589832 | tf_op jit(solution)/shard_map/ppermute | solution.py:295

commit v3 on v2

--- a/solution.py
+++ b/solution.py
@@ -17,6 +17,11 @@
 VMEM = pl.BlockSpec(memory_space=pltpu.VMEM)
 SMEM = pl.BlockSpec(memory_space=pltpu.SMEM)
 ANY = pl.BlockSpec(memory_space=pl.ANY)
+HBM = pl.BlockSpec(memory_space=pltpu.HBM)
+
+
+def in_hbm(array):
+    return pltpu.with_memory_space_constraint(array, pltpu.HBM)
 
 
 def in_vmem(array):
@@ -46,36 +51,45 @@
         wanted[owner] = jnp.broadcast_to(table[owner : owner + 1], wanted.shape[1:])
 
 
-def serve_kernel(peers, asked, factors, tiles, sent, table, first, listed, held, ready, sems):
+def prepare_kernel(factors, tiles, narrow, first, wide, sems):
+    whole = pltpu.make_async_copy(factors, wide, sems.at[0])
+    early = pltpu.make_async_copy(tiles.at[0], first, sems.at[1])
+    whole.start()
+    early.start()
+    whole.wait()
+    narrow[...] = wide[...].astype(narrow.dtype)
+    early.wait()
+
+
+def bring_kernel(ready, factors, kept, sem):
+    del ready
+    copy = pltpu.make_async_copy(factors, kept, sem)
+    copy.start()
+    copy.wait()
+
+
+def serve_kernel(peers, asked, narrow, sent, table, listed, ready, sems):
     copy = pltpu.make_async_copy(asked.at[:, 0, :], listed, sems.at[0])
     copy.start()
-    whole = pltpu.make_async_copy(factors, held, sems.at[6])
-    whole.start()
-    early = pltpu.make_async_copy(tiles.at[0], first, sems.at[1])
-    early.start()
     copy.wait()
     lane = lax.broadcasted_iota(jnp.int32, table.shape, 1)
     line = jnp.full(table.shape, -1, jnp.int32)
-    for peer in range(peers):
-        for rank in range(CAP):
-            line = jnp.where(lane == peer * CAP + rank, listed[peer, rank], line)
-    table[...] = line
-    whole.wait()
     group = peers // 4
     copies = []
     for peer in range(peers):
         for rank in range(CAP):
-            local = jnp.maximum(listed[peer, rank], 0)
-            ready[peer, rank * TILE : (rank + 1) * TILE, :] = held[local].astype(jnp.bfloat16)
+            local = listed[peer, rank]
+            line = jnp.where(lane == peer * CAP + rank, local, line)
+            ready[peer, rank * TILE : (rank + 1) * TILE, :] = narrow[jnp.maximum(local, 0)]
         if peer % group == group - 1:
             some = slice(peer + 1 - group, peer + 1)
             copies.append(
-                pltpu.make_async_copy(ready.at[some], sent.at[some], sems.at[2 + peer // group])
+                pltpu.make_async_copy(ready.at[some], sent.at[some], sems.at[1 + peer // group])
             )
             copies[-1].start()
+    table[...] = line
     for copy in copies:
         copy.wait()
-    early.wait()
 
 
 def tile_kernel(
@@ -103,23 +117,29 @@
             at = slice(i * TILE, (i + 1) * TILE)
             pair_ab[at, :] = (one[i : i + 1] * two).astype(bf16)
             pair_cd[at, :] = (three[i : i + 1] * four).astype(bf16)
-        outer = chunk // TILE
+        def spread(terms, first, other, kept):
+            terms = terms.reshape(-1, TILE, rank)
+            for i in range(terms.shape[0]):
+                kept = kept + terms[i] * first[i : i + 1]
+            return jnp.sum(terms * other[None], axis=1), kept
+
+        def left_of(at, kept):
+            left = jnp.dot(misfit[at : at + 2 * chunk, :], pair_cd[...], preferred_element_type=f32)
+            return spread(left, one[at // TILE : (at + 2 * chunk) // TILE], two, kept)
+
         grad_one, grad_two = [], jnp.zeros((TILE, rank), f32)
-        for at in range(0, EDGE, chunk):
+        for at in range(0, EDGE, 2 * chunk):
+            lines = slice(at, at + 2 * chunk)
             model = lax.dot_general(
-                pair_ab[at : at + chunk, :],
-                pair_cd[...],
-                (((1,), (1,)), ((), ())),
-                preferred_element_type=f32,
+                pair_ab[lines, :], pair_cd[...], (((1,), (1,)), ((), ())), preferred_element_type=f32
             )
-            off = (model - tile_at[at : at + chunk, :].astype(f32)).astype(bf16)
-            off = jnp.clip(off, jnp.asarray(-1.0, bf16), jnp.asarray(1.0, bf16))
-            misfit[at : at + chunk, :] = off
-            left = jnp.dot(off, pair_cd[...], preferred_element_type=f32).reshape(outer, TILE, rank)
-            grad_one.append(jnp.sum(left * two[None], axis=1))
-            for i in range(outer):
-                first = at // TILE + i
-                grad_two = grad_two + left[i] * one[first : first + 1]
+            off = (model - tile_at[lines, :].astype(f32)).astype(bf16)
+            misfit[lines, :] = jnp.clip(off, jnp.asarray(-1.0, bf16), jnp.asarray(1.0, bf16))
+            if at:
+                part_one, grad_two = left_of(at - 2 * chunk, grad_two)
+                grad_one.append(part_one)
+        part_one, grad_two = left_of(EDGE - 2 * chunk, grad_two)
+        grad_one.append(part_one)
         grad_three, grad_four = [], jnp.zeros((TILE, rank), f32)
         for at in range(0, EDGE, chunk):
             right = lax.dot_general(
@@ -127,11 +147,10 @@
                 pair_ab[...],
                 (((0,), (0,)), ((), ())),
                 preferred_element_type=f32,
-            ).reshape(outer, TILE, rank)
-            grad_three.append(jnp.sum(right * four[None], axis=1))
-            for k in range(outer):
-                first = at // TILE + k
-                grad_four = grad_four + right[k] * three[first : first + 1]
+            )
+            first = three[at // TILE : (at + chunk) // TILE]
+            part_three, grad_four = spread(right, first, four, grad_four)
+            grad_three.append(part_three)
         grads[names[0]] = jnp.concatenate(grad_one, 0)
         grads[names[1]] = grad_two
         grads[names[2]] = jnp.concatenate(grad_three, 0)
@@ -177,32 +196,23 @@
 
 
 def update_kernel(layer, factors, *refs):
-    own, other, (out, before, stepped, sems) = refs[:4], refs[4:8], refs[8:]
+    own, other, (out, stepped, sems) = refs[:4], refs[4:8], refs[8:]
     parts = len(own)
     height = TILE // parts
     held = factors.shape[0] // 4
-    modes = [slice(mode * held, (mode + 1) * held) for mode in range(4)]
-    brought = [
-        pltpu.make_async_copy(factors.at[blocks], before.at[blocks], sems.at[mode])
-        for mode, blocks in enumerate(modes)
-    ]
-    stored = [
-        pltpu.make_async_copy(stepped.at[blocks], out.at[blocks], sems.at[4 + mode])
-        for mode, blocks in enumerate(modes)
-    ]
-    for copy in brought:
-        copy.start()
-    for mode, blocks in enumerate(modes):
-        brought[mode].wait()
+    copies = []
+    for mode in range(4):
+        blocks = slice(mode * held, (mode + 1) * held)
         lines = slice(mode * held * height, (mode + 1) * held * height)
         for back in range(parts):
             source = lax.rem(layer[0] + parts - back, parts)
             at = pl.ds(pl.multiple_of(source * height, height), height)
             gradient = own[back][lines, :].astype(jnp.float32) + other[back][lines, :].astype(jnp.float32)
             gradient = gradient.reshape(held, height, -1)
-            stepped[blocks, at, :] = before[blocks, at, :] - step_size * gradient
-        stored[mode].start()
-    for copy in stored:
+            stepped[blocks, at, :] = factors[blocks, at, :] - step_size * gradient
+        copies.append(pltpu.make_async_copy(stepped.at[blocks], out.at[blocks], sems.at[mode]))
+        copies[-1].start()
+    for copy in copies:
         copy.wait()
 
 
@@ -215,6 +225,7 @@
     layer = (lax.axis_index("tiles") // 2).astype(jnp.int32).reshape(1)
     bf16, f32, i32 = jnp.bfloat16, jnp.float32, jnp.int32
 
+    small = pltpu.CompilerParams(vmem_limit_bytes=8 << 20)
     wanted, slots = pl.pallas_call(
         functools.partial(request_kernel, owners, blk_dev),
         out_shape=(
@@ -228,23 +239,32 @@
     )(tile_coords[0].T, tile_count)
     asked = lax.all_to_all(wanted, "rows", 0, 0)
 
-    sent, table, first = pl.pallas_call(
+    narrow, first = pl.pallas_call(
+        prepare_kernel,
+        out_shape=(pltpu.VMEM(factor_blocks.shape, bf16), pltpu.VMEM(tile_values.shape[2:], bf16)),
+        in_specs=[HBM, HBM],
+        out_specs=(VMEM, VMEM),
+        scratch_shapes=[pltpu.VMEM(factor_blocks.shape, f32), pltpu.SemaphoreType.DMA((2,))],
+        compiler_params=small,
+        cost_estimate=pl.CostEstimate(flops=0, bytes_accessed=4 << 20, transcendentals=0),
+        name="prepare",
+    )(in_hbm(factor_blocks), in_hbm(tile_values[0]))
+    sent, table = pl.pallas_call(
         functools.partial(serve_kernel, owners),
         out_shape=(
             jax.ShapeDtypeStruct((owners, CAP * TILE, rank), bf16),
             jax.ShapeDtypeStruct((8, LANES), i32),
-            pltpu.VMEM(tile_values.shape[2:], bf16),
         ),
-        in_specs=[ANY, ANY, ANY],
-        out_specs=(ANY, VMEM, VMEM),
+        in_specs=[ANY, VMEM],
+        out_specs=(ANY, VMEM),
         scratch_shapes=[
             pltpu.SMEM((owners, LANES), i32),
-            pltpu.VMEM(factor_blocks.shape, f32),
             pltpu.VMEM((owners, CAP * TILE, rank), bf16),
-            pltpu.SemaphoreType.DMA((7,)),
+            pltpu.SemaphoreType.DMA((5,)),
         ],
+        compiler_params=small,
         name="serve",
-    )(in_vmem(asked), factor_blocks, tile_values[0])
+    )(in_vmem(asked), in_vmem(narrow))
     blocks = lax.all_to_all(sent, "rows", 0, 0).reshape(owners * CAP * TILE, rank)
 
     def round_trip(back):
@@ -258,7 +278,7 @@
     messages = pl.pallas_call(
         functools.partial(tile_kernel, owners, layers, 256),
         out_shape=pltpu.VMEM((layers * owners, CAP * TILE // layers, rank), bf16),
-        in_specs=[SMEM, SMEM, VMEM, VMEM, ANY],
+        in_specs=[SMEM, SMEM, VMEM, VMEM, HBM],
         out_specs=VMEM,
         scratch_shapes=[
             pltpu.VMEM((slot_total, EDGE, EDGE), bf16),
@@ -268,12 +288,12 @@
             pltpu.VMEM((owners * CAP + 1, TILE, rank), f32),
             pltpu.SemaphoreType.DMA((slot_total,)),
         ],
-        compiler_params=pltpu.CompilerParams(vmem_limit_bytes=40 << 20),
+        compiler_params=pltpu.CompilerParams(vmem_limit_bytes=32 << 20),
         cost_estimate=pl.CostEstimate(
             flops=flops, bytes_accessed=2 * EDGE * EDGE * slot_total, transcendentals=0
         ),
         name="tiles",
-    )(tile_count, slots, in_vmem(blocks), in_vmem(first), tile_values[0])
+    )(tile_count, slots, in_vmem(blocks), in_vmem(first), in_hbm(tile_values[0]))
 
     same_core = [
         [t * owners + r for t in range(core, 2 * layers, 2) for r in range(owners)] for core in range(2)
@@ -287,6 +307,7 @@
         in_specs=[SMEM] * (1 + layers) + [VMEM],
         out_specs=VMEM,
         scratch_shapes=[pltpu.VMEM((held, height, rank), f32)] * CAP,
+        compiler_params=small,
         name="add",
     )(layer, *tables, in_vmem(came))
 
@@ -294,14 +315,25 @@
     pair = [(i, i ^ 1) for i in range(2 * layers)]
     other = [lax.ppermute(piece, "tiles", pair) for piece in own]
 
+    kept = pl.pallas_call(
+        bring_kernel,
+        out_shape=pltpu.VMEM(factor_blocks.shape, f32),
+        in_specs=[ANY, HBM],
+        out_specs=VMEM,
+        scratch_shapes=[pltpu.SemaphoreType.DMA],
+        compiler_params=small,
+        cost_estimate=pl.CostEstimate(flops=0, bytes_accessed=4 << 20, transcendentals=0),
+        name="bring",
+    )(partial, in_hbm(factor_blocks))
     updated = pl.pallas_call(
         update_kernel,
         out_shape=jax.ShapeDtypeStruct(factor_blocks.shape, f32),
-        in_specs=[SMEM, ANY] + [VMEM] * 8,
+        in_specs=[SMEM] + [VMEM] * 9,
         out_specs=ANY,
-        scratch_shapes=[pltpu.VMEM(factor_blocks.shape, f32)] * 2 + [pltpu.SemaphoreType.DMA((8,))],
+        scratch_shapes=[pltpu.VMEM(factor_blocks.shape, f32), pltpu.SemaphoreType.DMA((4,))],
+        compiler_params=small,
         name="update",
-    )(layer, factor_blocks, *[in_vmem(piece) for piece in own + other])
+    )(layer, in_vmem(kept), *[in_vmem(piece) for piece in own + other])
     return updated.reshape(factors.shape)
 
 

time: 99.5 us -> 97.2 us (0.977)
  blocking collectives: 38.5 us -> 25.1 us
  starting transfers between devices: 22 us -> 29.5 us
  waiting for transfers between devices: 11.8 us -> 14.9 us
    all_to_all x1 -> x0, blocking collectives: 14 us -> none  [on_device(): asked = lax.all_to_all(wanted, 'rows', 0, 0)]
    all_to_all x0 -> x1, starting transfers between devices: none -> 7.67 us  [on_device(): asked = lax.all_to_all(wanted, 'rows', 0, 0)]
    all_to_all x0 -> x1, waiting for transfers between devices: none -> 4.41 us  [on_device(): asked = lax.all_to_all(wanted, 'rows', 0, 0)]
    pallas_call x0 -> x2, Pallas kernels: none -> 3.51 us  [the longest x1 2.09 us: on_device(): pl.pallas_call(prepare_kernel, out_shape=(pltpu.VMEM(factor_blocks.shape,...]
    pallas_call x1, Pallas kernels: 3.05 us -> 1.69 us  [on_device(): pl.pallas_call(functools.partial(serve_kernel, owners), out_shape=(jax.Sh...]
    ppermute x4, waiting for transfers between devices: 1.07 us -> 0.01 us  [on_device(): other = [lax.ppermute(piece, 'tiles', pair) for piece in own]]
    pallas_call x1, Pallas kernels: 2.27 us -> 1.25 us  [on_device(): pl.pallas_call(update_kernel, out_shape=jax.ShapeDtypeStruct(factor_block...]
  transfers between devices with their start and end apart: 11 -> 12, of which waited for: 4 -> 3; matrix products, arithmetic and copies ran while one was open for 0% -> 0% of each run, Pallas kernels for 0% -> 4%
where the time goes in v3:
time: 97.2 us; the launch traced here: 96.7 us
  starting transfers between devices  29.5 us (30%)
  Pallas kernels  26.5 us (27%)
  blocking collectives  25.1 us (26%)
  waiting for transfers between devices  14.9 us (15%)
    all_to_all x1, blocking collectives, on_device(): lax.all_to_all(messages, ('tiles', 'rows'), 0, 0, axis_index_groups=same_...  25.1 us
    pallas_call x1, Pallas kernels, on_device(): pl.pallas_call(functools.partial(tile_kernel, owners, layers, 256), out_s...  17 us
    ppermute x4, starting transfers between devices, on_device(): other = [lax.ppermute(piece, 'tiles', pair) for piece in own]  11.6 us
    all_to_all x1, starting transfers between devices, on_device(): asked = lax.all_to_all(wanted, 'rows', 0, 0)  7.67 us
    all_to_all x1, waiting for transfers between devices, on_device(): lax.all_to_all(sent, 'rows', 0, 0).reshape(owners * CAP * TILE, rank)  7.24 us
    ppermute x3, starting transfers between devices, on_device(): lax.ppermute(table, 'tiles', round_trip(back))  4.49 us
    all_to_all x1, waiting for transfers between devices, on_device(): asked = lax.all_to_all(wanted, 'rows', 0, 0)  4.41 us
    all_to_all x1, starting transfers between devices, on_device(): lax.all_to_all(sent, 'rows', 0, 0).reshape(owners * CAP * TILE, rank)  3.67 us
  transfers between devices with their start and end apart: 12, of which 3 were waited for; matrix products, arithmetic and copies ran while one was open for 0% of the time, Pallas kernels for 4%

profile of v3, /device:TPU:1, one launch (start us, length us, event | category | flops | bytes accessed | tf_op | source)
XLA Modules:
  0.0 96.7 jit_solution(14931791750603700999)
XLA Ops:
  0.7 1.6 %requests.1 = (s32[16,8,128]{2,1,0:T(8,128)}, s32[32]{0:T(128)}) custom-call(s32[4,8]{1,0:T(4,128)} %bitcast.13, s32[1]{0:T(128)S(6)} %copy.5.count), custom_call_target="tpu_custom_call" | custom-call | tf_op jit(solution)/shard_map/requests/pallas_call | solution.py:229
  2.2 7.7 %all-to-all-start = ((s32[16,8,128]{2,1,0:T(8,128)}), s32[16,8,128]{2,1,0:T(8,128)S(1)}, u32[]{:S(2)}, u32[]{:S(2)}) async-start(s32[16,8,128]{2,1,0:T(8,128)} %get-tuple-element.18), calls=%async_computation | async-start | bytes 131072 | tf_op jit(solution)/shard_map/all_to_all | solution.py:240
  9.9 2.1 %prepare.1 = (bf16[48,32,256]{2,1,0:T(8,128)(2,1)S(1)}, bf16[1024,1024]{1,0:T(8,128)(2,1)S(1)}) custom-call(f32[48,32,256]{2,1,0:T(8,128)} %bitcast.11, bf16[8,1024,1024]{2,1,0:T(8,128)(2,1)} %bitcast.9), custom_call_target="tpu_custom_call" | custom-call | bytes 4194304 | tf_op jit(solution)/shard_map/prepare/pallas_call | solution.py:242
  12.0 4.4 %all-to-all-done.asked = s32[16,8,128]{2,1,0:T(8,128)S(1)} async-done(((s32[16,8,128]{2,1,0:T(8,128)}), s32[16,8,128]{2,1,0:T(8,128)S(1)}, u32[]{:S(2)}, u32[]{:S(2)}) %all-to-all-start) | async-done | bytes 65568 | tf_op jit(solution)/shard_map/all_to_all | solution.py:240
  16.4 1.7 %serve.1 = (bf16[16,128,256]{2,1,0:T(8,128)(2,1)}, s32[8,128]{1,0:T(8,128)S(1)}) custom-call(s32[16,8,128]{2,1,0:T(8,128)S(1)} %all-to-all-done.asked, bf16[48,32,256]{2,1,0:T(8,128)(2,1)S(1)} %get-tuple-element.19.narrow), custom_call_target="tpu_custom_call" | custom-call | tf_op jit(solution)/shard_map/serve/pallas_call | solution.py:252
  18.1 3.7 %all-to-all-start.1 = ((bf16[16,128,256]{2,1,0:T(8,128)(2,1)}), bf16[16,128,256]{2,1,0:T(8,128)(2,1)S(1)}, u32[]{:S(2)}, u32[]{:S(2)}) async-start(bf16[16,128,256]{2,1,0:T(8,128)(2,1)} %get-tuple-element.27), calls=%async_computation.1 | async-start | bytes 2097152 | tf_op jit(solution)/shard_map/all_to_all | solution.py:268
  21.8 3.7 %collective-permute-start.2 = (s32[8,128]{1,0:T(8,128)S(1)}, s32[8,128]{1,0:T(8,128)S(1)}, u32[]{:S(2)}, u32[]{:S(2)}) collective-permute-start(s32[8,128]{1,0:T(8,128)S(1)} %get-tuple-element.22.table_0), channel_id=1, source_target_pairs={{0,96},{16,112},{32,0},{48,16},{64,32},{80,48},{96,64},{112,80},{1... | collective-permute-start | bytes 12296 | tf_op jit(solution)/shard_map/ppermute | solution.py:274
  25.5 0.0 collective-permute-start.1
  25.5 0.8 collective-permute-start
  26.3 0.0 collective-permute-done.2.table_3
  26.3 3.2 %collective-permute-done.1.table_2 = s32[8,128]{1,0:T(8,128)S(1)} collective-permute-done((s32[8,128]{1,0:T(8,128)S(1)}, s32[8,128]{1,0:T(8,128)S(1)}, u32[]{:S(2)}, u32[]{:S(2)}) %collective-permute-start.1) | collective-permute-done | bytes 4128 | tf_op jit(solution)/shard_map/ppermute | solution.py:274
  29.5 0.0 collective-permute-done.table_1
  29.5 7.2 %all-to-all-done.1 = bf16[16,128,256]{2,1,0:T(8,128)(2,1)S(1)} async-done(((bf16[16,128,256]{2,1,0:T(8,128)(2,1)}), bf16[16,128,256]{2,1,0:T(8,128)(2,1)S(1)}, u32[]{:S(2)}, u32[]{:S(2)}) %all-to-all-start.1) | async-done | bytes 1048608 | tf_op jit(solution)/shard_map/all_to_all | solution.py:268
  36.7 17.0 %tiles.1 = bf16[64,32,256]{2,1,0:T(8,128)(2,1)S(1)} custom-call(s32[1]{0:T(128)S(6)} %copy.5.count, s32[32]{0:T(128)S(1)} %copy-done, bf16[2048,256]{1,0:T(8,128)(2,1)S(1)} %bitcast.8, bf16[1024,1024]{1,0:T(8,128)(2,1)S(1)} %get-tuple-element.28.early, bf16[8,1024,1024]{2,1,0:T(8,128)(2,1)} %bitcast.10), custom_call_target="tpu_custom_call" | custom-call | flops 12884901888 | bytes 16777216 | tf_op jit(solution)/shard_map/tiles/pallas_call | solution.py:278
  53.7 25.1 %all_to_all.15.came = bf16[64,32,256]{2,1,0:T(8,128)(2,1)S(1)} all-to-all(bf16[64,32,256]{2,1,0:T(8,128)(2,1)S(1)} %tiles.1), channel_id=1, replica_groups={{0,1,2,3,4,5,6,7,8,9,10,11,12,13,14,15,32,33,34,35,36,37,38,39,40,41,42..., dimensions={0} | all-to-all | bytes 2097152 | tf_op jit(solution)/shard_map/all_to_all | solution.py:301
  78.8 1.5 %add.2.ready.refs_0_ = bf16[384,256]{1,0:T(8,128)(2,1)S(1)} custom-call(s32[1]{0:T(128)} %bitcast.4.layer, s32[8,128]{1,0:T(8,128)S(1)} %get-tuple-element.22.table_0, s32[8,128]{1,0:T(8,128)S(1)} %collective-permute-done.table_1, s32[8,128]{1,0:T(8,128)S(1)} %collective-permute-done.1.table_2, s32[8,128]{1,0:T(8,128)S(1)} %collective-permute-done.2.table_3, ...), custom_call_target="tpu_custom_call" | custom-call | tf_op jit(solution)/shard_map/add/pallas_call | solution.py:304
  80.3 0.6 collective-permute-start.5
  81.0 1.4 %collective-permute-start.4 = (bf16[384,256]{1,0:T(8,128)(2,1)S(1)}, bf16[384,256]{1,0:T(8,128)(2,1)S(1)}, u32[]{:S(2)}, u32[]{:S(2)}) collective-permute-start(bf16[384,256]{1,0:T(8,128)(2,1)S(1)} %add.2.ready.refs_0_), channel_id=1, source_target_pairs={{0,64},{16,80},{32,96},{48,112},{64,0},{80,16},{96,32},{112,48},{1... | collective-permute-start | bytes 589832 | tf_op jit(solution)/shard_map/ppermute | solution.py:314
  82.3 0.0 collective-permute-start.3
  82.3 3.8 %collective-permute-start.6 = (bf16[384,256]{1,0:T(8,128)(2,1)S(1)}, bf16[384,256]{1,0:T(8,128)(2,1)S(1)}, u32[]{:S(2)}, u32[]{:S(2)}) collective-permute-start(bf16[384,256]{1,0:T(8,128)(2,1)S(1)} %add.2.ready.refs_0_), channel_id=1, source_target_pairs={{0,16},{16,0},{32,48},{48,32},{64,80},{80,64},{96,112},{112,96},{1... | collective-permute-start | bytes 589832 | tf_op jit(solution)/shard_map/ppermute | solution.py:316
  86.1 0.0 collective-permute-done.5.refs_3_
  86.1 3.7 %collective-permute-start.9 = (bf16[384,256]{1,0:T(8,128)(2,1)S(1)}, bf16[384,256]{1,0:T(8,128)(2,1)S(1)}, u32[]{:S(2)}, u32[]{:S(2)}) collective-permute-start(bf16[384,256]{1,0:T(8,128)(2,1)S(1)} %collective-permute-done.5.refs_3_), channel_id=1, source_target_pairs={{0,16},{16,0},{32,48},{48,32},{64,80},{80,64},{96,112},{112,96},{1... | collective-permute-start | bytes 589832 | tf_op jit(solution)/shard_map/ppermute | solution.py:316
  89.8 0.0 collective-permute-done.4.refs_2_
  89.8 2.2 %collective-permute-start.8 = (bf16[384,256]{1,0:T(8,128)(2,1)S(1)}, bf16[384,256]{1,0:T(8,128)(2,1)S(1)}, u32[]{:S(2)}, u32[]{:S(2)}) collective-permute-start(bf16[384,256]{1,0:T(8,128)(2,1)S(1)} %collective-permute-done.4.refs_2_), channel_id=1, source_target_pairs={{0,16},{16,0},{32,48},{48,32},{64,80},{80,64},{96,112},{112,96},{1... | collective-permute-start | bytes 589832 | tf_op jit(solution)/shard_map/ppermute | solution.py:316
  92.0 0.0 collective-permute-done.3.refs_1_
  92.0 2.0 %collective-permute-start.7 = (bf16[384,256]{1,0:T(8,128)(2,1)S(1)}, bf16[384,256]{1,0:T(8,128)(2,1)S(1)}, u32[]{:S(2)}, u32[]{:S(2)}) collective-permute-start(bf16[384,256]{1,0:T(8,128)(2,1)S(1)} %collective-permute-done.3.refs_1_), channel_id=1, source_target_pairs={{0,16},{16,0},{32,48},{48,32},{64,80},{80,64},{96,112},{112,96},{1... | collective-permute-start | bytes 589832 | tf_op jit(solution)/shard_map/ppermute | solution.py:316
  94.0 1.4 %bring.1.factors = f32[48,32,256]{2,1,0:T(8,128)S(1)} custom-call(bf16[384,256]{1,0:T(8,128)(2,1)S(1)} %add.2.ready.refs_0_, f32[48,32,256]{2,1,0:T(8,128)} %bitcast.12), custom_call_target="tpu_custom_call" | custom-call | bytes 4194304 | tf_op jit(solution)/shard_map/bring/pallas_call | solution.py:318
  95.4 0.0 collective-permute-done.6.refs_4_
  95.4 0.0 collective-permute-done.9.refs_7_
  95.4 0.0 collective-permute-done.8.refs_6_
  95.4 0.0 collective-permute-done.7.refs_5_
  95.5 1.2 %update.1 = f32[48,32,256]{2,1,0:T(8,128)} custom-call(s32[1]{0:T(128)} %bitcast.4.layer, f32[48,32,256]{2,1,0:T(8,128)S(1)} %bring.1.factors, bf16[384,256]{1,0:T(8,128)(2,1)S(1)} %add.2.ready.refs_0_, bf16[384,256]{1,0:T(8,128)(2,1)S(1)} %collective-permute-done.3.refs_1_, bf16[384,256]{1,0:T(8,128)(2,1)S(1)} %collective-permute-done.4.refs_2_, ...), custom_call_target="tpu_custom_call" | custom-call | tf_op jit(solution)/shard_map/update/pallas_call | solution.py:328
  (2 shorter events, 0.0 us)
Async XLA Ops:
  2.2 14.2 %all-to-all-start = ((s32[16,8,128]{2,1,0:T(8,128)}), s32[16,8,128]{2,1,0:T(8,128)S(1)}, u32[]{:S(2)}, u32[]{:S(2)}) async-start(s32[16,8,128]{2,1,0:T(8,128)} %get-tuple-element.18), calls=%async_computation | async-start | bytes 131072 | tf_op jit(solution)/shard_map/all_to_all | solution.py:240
  12.0 24.7 %copy-start = (s32[32]{0:T(128)S(1)}, s32[32]{0:T(128)}, u32[]{:S(2)}) copy-start(s32[32]{0:T(128)} %get-tuple-element.26.slots) | copy-start | bytes 388
  18.1 18.6 %all-to-all-start.1 = ((bf16[16,128,256]{2,1,0:T(8,128)(2,1)}), bf16[16,128,256]{2,1,0:T(8,128)(2,1)S(1)}, u32[]{:S(2)}, u32[]{:S(2)}) async-start(bf16[16,128,256]{2,1,0:T(8,128)(2,1)} %get-tuple-element.27), calls=%async_computation.1 | async-start | bytes 2097152 | tf_op jit(solution)/shard_map/all_to_all | solution.py:268
  21.8 4.5 %collective-permute-start.2 = (s32[8,128]{1,0:T(8,128)S(1)}, s32[8,128]{1,0:T(8,128)S(1)}, u32[]{:S(2)}, u32[]{:S(2)}) collective-permute-start(s32[8,128]{1,0:T(8,128)S(1)} %get-tuple-element.22.table_0), channel_id=1, source_target_pairs={{0,96},{16,112},{32,0},{48,16},{64,32},{80,48},{96,64},{112,80},{1... | collective-permute-start | bytes 12296 | tf_op jit(solution)/shard_map/ppermute | solution.py:274
  25.5 4.0 %collective-permute-start.1 = (s32[8,128]{1,0:T(8,128)S(1)}, s32[8,128]{1,0:T(8,128)S(1)}, u32[]{:S(2)}, u32[]{:S(2)}) collective-permute-start(s32[8,128]{1,0:T(8,128)S(1)} %get-tuple-element.22.table_0), channel_id=1, source_target_pairs={{0,64},{16,80},{32,96},{48,112},{64,0},{80,16},{96,32},{112,48},{1... | collective-permute-start | bytes 12296 | tf_op jit(solution)/shard_map/ppermute | solution.py:274
  25.5 4.0 %collective-permute-start = (s32[8,128]{1,0:T(8,128)S(1)}, s32[8,128]{1,0:T(8,128)S(1)}, u32[]{:S(2)}, u32[]{:S(2)}) collective-permute-start(s32[8,128]{1,0:T(8,128)S(1)} %get-tuple-element.22.table_0), channel_id=1, source_target_pairs={{0,32},{16,48},{32,64},{48,80},{64,96},{80,112},{96,0},{112,16},{1... | collective-permute-start | bytes 12296 | tf_op jit(solution)/shard_map/ppermute | solution.py:274
  80.3 5.8 %collective-permute-start.5 = (bf16[384,256]{1,0:T(8,128)(2,1)S(1)}, bf16[384,256]{1,0:T(8,128)(2,1)S(1)}, u32[]{:S(2)}, u32[]{:S(2)}) collective-permute-start(bf16[384,256]{1,0:T(8,128)(2,1)S(1)} %add.2.ready.refs_0_), channel_id=1, source_target_pairs={{0,96},{16,112},{32,0},{48,16},{64,32},{80,48},{96,64},{112,80},{1... | collective-permute-start | bytes 589832 | tf_op jit(solution)/shard_map/ppermute | solution.py:314
  81.0 8.9 %collective-permute-start.4 = (bf16[384,256]{1,0:T(8,128)(2,1)S(1)}, bf16[384,256]{1,0:T(8,128)(2,1)S(1)}, u32[]{:S(2)}, u32[]{:S(2)}) collective-permute-start(bf16[384,256]{1,0:T(8,128)(2,1)S(1)} %add.2.ready.refs_0_), channel_id=1, source_target_pairs={{0,64},{16,80},{32,96},{48,112},{64,0},{80,16},{96,32},{112,48},{1... | collective-permute-start | bytes 589832 | tf_op jit(solution)/shard_map/ppermute | solution.py:314
  82.3 9.7 %collective-permute-start.3 = (bf16[384,256]{1,0:T(8,128)(2,1)S(1)}, bf16[384,256]{1,0:T(8,128)(2,1)S(1)}, u32[]{:S(2)}, u32[]{:S(2)}) collective-permute-start(bf16[384,256]{1,0:T(8,128)(2,1)S(1)} %add.2.ready.refs_0_), channel_id=1, source_target_pairs={{0,32},{16,48},{32,64},{48,80},{64,96},{80,112},{96,0},{112,16},{1... | collective-permute-start | bytes 589832 | tf_op jit(solution)/shard_map/ppermute | solution.py:314
  82.3 13.1 %collective-permute-start.6 = (bf16[384,256]{1,0:T(8,128)(2,1)S(1)}, bf16[384,256]{1,0:T(8,128)(2,1)S(1)}, u32[]{:S(2)}, u32[]{:S(2)}) collective-permute-start(bf16[384,256]{1,0:T(8,128)(2,1)S(1)} %add.2.ready.refs_0_), channel_id=1, source_target_pairs={{0,16},{16,0},{32,48},{48,32},{64,80},{80,64},{96,112},{112,96},{1... | collective-permute-start | bytes 589832 | tf_op jit(solution)/shard_map/ppermute | solution.py:316
  86.1 9.3 %collective-permute-start.9 = (bf16[384,256]{1,0:T(8,128)(2,1)S(1)}, bf16[384,256]{1,0:T(8,128)(2,1)S(1)}, u32[]{:S(2)}, u32[]{:S(2)}) collective-permute-start(bf16[384,256]{1,0:T(8,128)(2,1)S(1)} %collective-permute-done.5.refs_3_), channel_id=1, source_target_pairs={{0,16},{16,0},{32,48},{48,32},{64,80},{80,64},{96,112},{112,96},{1... | collective-permute-start | bytes 589832 | tf_op jit(solution)/shard_map/ppermute | solution.py:316
  89.8 5.6 %collective-permute-start.8 = (bf16[384,256]{1,0:T(8,128)(2,1)S(1)}, bf16[384,256]{1,0:T(8,128)(2,1)S(1)}, u32[]{:S(2)}, u32[]{:S(2)}) collective-permute-start(bf16[384,256]{1,0:T(8,128)(2,1)S(1)} %collective-permute-done.4.refs_2_), channel_id=1, source_target_pairs={{0,16},{16,0},{32,48},{48,32},{64,80},{80,64},{96,112},{112,96},{1... | collective-permute-start | bytes 589832 | tf_op jit(solution)/shard_map/ppermute | solution.py:316
  92.0 3.5 %collective-permute-start.7 = (bf16[384,256]{1,0:T(8,128)(2,1)S(1)}, bf16[384,256]{1,0:T(8,128)(2,1)S(1)}, u32[]{:S(2)}, u32[]{:S(2)}) collective-permute-start(bf16[384,256]{1,0:T(8,128)(2,1)S(1)} %collective-permute-done.3.refs_1_), channel_id=1, source_target_pairs={{0,16},{16,0},{32,48},{48,32},{64,80},{80,64},{96,112},{112,96},{1... | collective-permute-start | bytes 589832 | tf_op jit(solution)/shard_map/ppermute | solution.py:316

commit v4 on v3

--- a/solution.py
+++ b/solution.py
@@ -98,19 +98,22 @@
     live, total = count[0], tiles.shape[0]
     f32, bf16 = jnp.float32, jnp.bfloat16
     rank = blocks.shape[-1]
-    spare = owners * CAP
 
     def fetch(slot):
         return pltpu.make_async_copy(tiles.at[slot], values.at[slot], sems.at[slot])
 
     for slot in range(1, total):
-        fetch(slot).start()
+
+        @pl.when(slot < live)
+        def _():
+            fetch(slot).start()
+
     grads[...] = jnp.zeros_like(grads)
 
     def tile(slot, tile_at):
-        names = [jnp.where(slot < live, slots[slot * 4 + mode], spare) for mode in range(4)]
+        names = [slots[slot * 4 + mode] for mode in range(4)]
         one, two, three, four = [
-            blocks[pl.ds(pl.multiple_of(jnp.minimum(name, spare - 1) * TILE, TILE), TILE), :].astype(f32)
+            blocks[pl.ds(pl.multiple_of(name * TILE, TILE), TILE), :].astype(f32)
             for name in names
         ]
         for i in range(TILE):
@@ -162,7 +165,7 @@
         return carry
 
     tile(0, early)
-    lax.fori_loop(1, total, later, 0)
+    lax.fori_loop(1, live, later, 0)
     height = TILE // parts
     for owner in range(owners):
         for part in range(parts):
@@ -285,7 +288,7 @@
             pltpu.VMEM((EDGE, EDGE), bf16),
             pltpu.VMEM((EDGE, rank), bf16),
             pltpu.VMEM((EDGE, rank), bf16),
-            pltpu.VMEM((owners * CAP + 1, TILE, rank), f32),
+            pltpu.VMEM((owners * CAP, TILE, rank), f32),
             pltpu.SemaphoreType.DMA((slot_total,)),
         ],
         compiler_params=pltpu.CompilerParams(vmem_limit_bytes=32 << 20),
@@ -313,8 +316,6 @@
 
     own = [partial] + [lax.ppermute(partial, "tiles", round_trip(back)) for back in range(1, layers)]
     pair = [(i, i ^ 1) for i in range(2 * layers)]
-    other = [lax.ppermute(piece, "tiles", pair) for piece in own]
-
     kept = pl.pallas_call(
         bring_kernel,
         out_shape=pltpu.VMEM(factor_blocks.shape, f32),
@@ -325,6 +326,9 @@
         cost_estimate=pl.CostEstimate(flops=0, bytes_accessed=4 << 20, transcendentals=0),
         name="bring",
     )(partial, in_hbm(factor_blocks))
+    here, kept = lax.optimization_barrier((partial, kept))
+    other = [lax.ppermute(piece, "tiles", pair) for piece in [here] + own[1:]]
+
     updated = pl.pallas_call(
         update_kernel,
         out_shape=jax.ShapeDtypeStruct(factor_blocks.shape, f32),

time: 97.2 us -> 96 us (0.988); the launches traced: 96.7 us -> 94.4 us
  Pallas kernels: 26.5 us -> 18.3 us
  blocking collectives: 25.1 us -> 30.6 us
  waiting for transfers between devices: 14.9 us -> 16.1 us
    pallas_call x1, Pallas kernels: 17 us -> 8.87 us  [on_device(): pl.pallas_call(functools.partial(tile_kernel, owners, layers, 256), out_s...]
    all_to_all x1, blocking collectives: 25.1 us -> 30.6 us  [on_device(): lax.all_to_all(messages, ('tiles', 'rows'), 0, 0, axis_index_groups=same_...]
    ppermute x4, waiting for transfers between devices: 0.01 us -> 1.07 us  [on_device(): other = [lax.ppermute(piece, 'tiles', pair) for piece in [here] + own[1:]]]
  transfers between devices with their start and end apart: 12 -> 12, of which waited for: 3 -> 4; matrix products, arithmetic and copies ran while one was open for 0% -> 0% of each run, Pallas kernels for 4% -> 4%
where the time goes in v4:
time: 96 us; the launch traced here: 94.4 us
  blocking collectives  30.6 us (32%)
  starting transfers between devices  28.7 us (30%)
  Pallas kernels  18.3 us (19%)
  waiting for transfers between devices  16.1 us (17%)
    all_to_all x1, blocking collectives, on_device(): lax.all_to_all(messages, ('tiles', 'rows'), 0, 0, axis_index_groups=same_...  30.6 us
    ppermute x4, starting transfers between devices, on_device(): other = [lax.ppermute(piece, 'tiles', pair) for piece in [here] + own[1:]]  11.3 us
    pallas_call x1, Pallas kernels, on_device(): pl.pallas_call(functools.partial(tile_kernel, owners, layers, 256), out_s...  8.87 us
    all_to_all x1, starting transfers between devices, on_device(): asked = lax.all_to_all(wanted, 'rows', 0, 0)  7.67 us
    all_to_all x1, waiting for transfers between devices, on_device(): lax.all_to_all(sent, 'rows', 0, 0).reshape(owners * CAP * TILE, rank)  7.36 us
    ppermute x3, starting transfers between devices, on_device(): lax.ppermute(table, 'tiles', round_trip(back))  4.49 us
    all_to_all x1, waiting for transfers between devices, on_device(): asked = lax.all_to_all(wanted, 'rows', 0, 0)  4.45 us
    all_to_all x1, starting transfers between devices, on_device(): lax.all_to_all(sent, 'rows', 0, 0).reshape(owners * CAP * TILE, rank)  3.67 us
  transfers between devices with their start and end apart: 12, of which 4 were waited for; matrix products, arithmetic and copies ran while one was open for 0% of the time, Pallas kernels for 4%

profile of v4, /device:TPU:1, one launch (start us, length us, event | category | flops | bytes accessed | tf_op | source)
XLA Modules:
  0.0 94.4 jit_solution(15143821591851780837)
XLA Ops:
  0.7 1.5 %requests.1 = (s32[16,8,128]{2,1,0:T(8,128)}, s32[32]{0:T(128)}) custom-call(s32[4,8]{1,0:T(4,128)} %bitcast.13, s32[1]{0:T(128)S(6)} %copy.5.count), custom_call_target="tpu_custom_call" | custom-call | tf_op jit(solution)/shard_map/requests/pallas_call | solution.py:232
  2.2 7.7 %all-to-all-start = ((s32[16,8,128]{2,1,0:T(8,128)}), s32[16,8,128]{2,1,0:T(8,128)S(1)}, u32[]{:S(2)}, u32[]{:S(2)}) async-start(s32[16,8,128]{2,1,0:T(8,128)} %get-tuple-element.20), calls=%async_computation | async-start | bytes 131072 | tf_op jit(solution)/shard_map/all_to_all | solution.py:243
  9.8 2.1 %prepare.1 = (bf16[48,32,256]{2,1,0:T(8,128)(2,1)S(1)}, bf16[1024,1024]{1,0:T(8,128)(2,1)S(1)}) custom-call(f32[48,32,256]{2,1,0:T(8,128)} %bitcast.11, bf16[8,1024,1024]{2,1,0:T(8,128)(2,1)} %bitcast.9), custom_call_target="tpu_custom_call" | custom-call | bytes 4194304 | tf_op jit(solution)/shard_map/prepare/pallas_call | solution.py:245
  11.9 4.4 %all-to-all-done.asked = s32[16,8,128]{2,1,0:T(8,128)S(1)} async-done(((s32[16,8,128]{2,1,0:T(8,128)}), s32[16,8,128]{2,1,0:T(8,128)S(1)}, u32[]{:S(2)}, u32[]{:S(2)}) %all-to-all-start) | async-done | bytes 65568 | tf_op jit(solution)/shard_map/all_to_all | solution.py:243
  16.4 1.7 %serve.1 = (bf16[16,128,256]{2,1,0:T(8,128)(2,1)}, s32[8,128]{1,0:T(8,128)S(1)}) custom-call(s32[16,8,128]{2,1,0:T(8,128)S(1)} %all-to-all-done.asked, bf16[48,32,256]{2,1,0:T(8,128)(2,1)S(1)} %get-tuple-element.21.narrow), custom_call_target="tpu_custom_call" | custom-call | tf_op jit(solution)/shard_map/serve/pallas_call | solution.py:255
  18.1 3.7 %all-to-all-start.1 = ((bf16[16,128,256]{2,1,0:T(8,128)(2,1)}), bf16[16,128,256]{2,1,0:T(8,128)(2,1)S(1)}, u32[]{:S(2)}, u32[]{:S(2)}) async-start(bf16[16,128,256]{2,1,0:T(8,128)(2,1)} %get-tuple-element.29), calls=%async_computation.1 | async-start | bytes 2097152 | tf_op jit(solution)/shard_map/all_to_all | solution.py:271
  21.8 3.7 %collective-permute-start.2 = (s32[8,128]{1,0:T(8,128)S(1)}, s32[8,128]{1,0:T(8,128)S(1)}, u32[]{:S(2)}, u32[]{:S(2)}) collective-permute-start(s32[8,128]{1,0:T(8,128)S(1)} %get-tuple-element.24.table_0), channel_id=1, source_target_pairs={{0,96},{16,112},{32,0},{48,16},{64,32},{80,48},{96,64},{112,80},{1... | collective-permute-start | bytes 12296 | tf_op jit(solution)/shard_map/ppermute | solution.py:277
  25.5 0.0 collective-permute-start.1
  25.5 0.8 collective-permute-start
  26.3 0.0 collective-permute-done.2.table_3
  26.3 3.2 %collective-permute-done.1.table_2 = s32[8,128]{1,0:T(8,128)S(1)} collective-permute-done((s32[8,128]{1,0:T(8,128)S(1)}, s32[8,128]{1,0:T(8,128)S(1)}, u32[]{:S(2)}, u32[]{:S(2)}) %collective-permute-start.1) | collective-permute-done | bytes 4128 | tf_op jit(solution)/shard_map/ppermute | solution.py:277
  29.4 0.0 collective-permute-done.table_1
  29.5 7.4 %all-to-all-done.1 = bf16[16,128,256]{2,1,0:T(8,128)(2,1)S(1)} async-done(((bf16[16,128,256]{2,1,0:T(8,128)(2,1)}), bf16[16,128,256]{2,1,0:T(8,128)(2,1)S(1)}, u32[]{:S(2)}, u32[]{:S(2)}) %all-to-all-start.1) | async-done | bytes 1048608 | tf_op jit(solution)/shard_map/all_to_all | solution.py:271
  36.8 8.9 %tiles.1 = bf16[64,32,256]{2,1,0:T(8,128)(2,1)S(1)} custom-call(s32[1]{0:T(128)S(6)} %copy.5.count, s32[32]{0:T(128)S(1)} %copy-done, bf16[2048,256]{1,0:T(8,128)(2,1)S(1)} %bitcast.8, bf16[1024,1024]{1,0:T(8,128)(2,1)S(1)} %get-tuple-element.30.early, bf16[8,1024,1024]{2,1,0:T(8,128)(2,1)} %bitcast.10), custom_call_target="tpu_custom_call" | custom-call | flops 12884901888 | bytes 16777216 | tf_op jit(solution)/shard_map/tiles/pallas_call | solution.py:281
  45.7 30.6 %all_to_all.15.came = bf16[64,32,256]{2,1,0:T(8,128)(2,1)S(1)} all-to-all(bf16[64,32,256]{2,1,0:T(8,128)(2,1)S(1)} %tiles.1), channel_id=1, replica_groups={{0,1,2,3,4,5,6,7,8,9,10,11,12,13,14,15,32,33,34,35,36,37,38,39,40,41,42..., dimensions={0} | all-to-all | bytes 2097152 | tf_op jit(solution)/shard_map/all_to_all | solution.py:304
  76.3 1.5 %add.2.ready.refs_0_ = bf16[384,256]{1,0:T(8,128)(2,1)S(1)} custom-call(s32[1]{0:T(128)} %bitcast.4.layer, s32[8,128]{1,0:T(8,128)S(1)} %get-tuple-element.24.table_0, s32[8,128]{1,0:T(8,128)S(1)} %collective-permute-done.table_1, s32[8,128]{1,0:T(8,128)S(1)} %collective-permute-done.1.table_2, s32[8,128]{1,0:T(8,128)S(1)} %collective-permute-done.2.table_3, ...), custom_call_target="tpu_custom_call" | custom-call | tf_op jit(solution)/shard_map/add/pallas_call | solution.py:307
  77.8 0.7 collective-permute-start.5
  78.5 0.9 collective-permute-start.4
  79.4 0.0 collective-permute-start.3
  79.4 1.4 %bring.1.factors = f32[48,32,256]{2,1,0:T(8,128)S(1)} custom-call(bf16[384,256]{1,0:T(8,128)(2,1)S(1)} %add.2.ready.refs_0_, f32[48,32,256]{2,1,0:T(8,128)} %bitcast.12), custom_call_target="tpu_custom_call" | custom-call | bytes 4194304 | tf_op jit(solution)/shard_map/bring/pallas_call | solution.py:319
  80.8 5.2 %collective-permute-start.6 = (bf16[384,256]{1,0:T(8,128)(2,1)S(1)}, bf16[384,256]{1,0:T(8,128)(2,1)S(1)}, u32[]{:S(2)}, u32[]{:S(2)}) collective-permute-start(bf16[384,256]{1,0:T(8,128)(2,1)S(1)} %add.2.ready.refs_0_), channel_id=1, source_target_pairs={{0,16},{16,0},{32,48},{48,32},{64,80},{80,64},{96,112},{112,96},{1... | collective-permute-start | bytes 589832 | tf_op jit(solution)/shard_map/ppermute | solution.py:330
  86.0 0.0 collective-permute-done.5.refs_3_
  86.0 1.7 %collective-permute-start.9 = (bf16[384,256]{1,0:T(8,128)(2,1)S(1)}, bf16[384,256]{1,0:T(8,128)(2,1)S(1)}, u32[]{:S(2)}, u32[]{:S(2)}) collective-permute-start(bf16[384,256]{1,0:T(8,128)(2,1)S(1)} %collective-permute-done.5.refs_3_), channel_id=1, source_target_pairs={{0,16},{16,0},{32,48},{48,32},{64,80},{80,64},{96,112},{112,96},{1... | collective-permute-start | bytes 589832 | tf_op jit(solution)/shard_map/ppermute | solution.py:330
  87.7 0.0 collective-permute-done.4.refs_2_
  87.7 2.4 %collective-permute-start.8 = (bf16[384,256]{1,0:T(8,128)(2,1)S(1)}, bf16[384,256]{1,0:T(8,128)(2,1)S(1)}, u32[]{:S(2)}, u32[]{:S(2)}) collective-permute-start(bf16[384,256]{1,0:T(8,128)(2,1)S(1)} %collective-permute-done.4.refs_2_), channel_id=1, source_target_pairs={{0,16},{16,0},{32,48},{48,32},{64,80},{80,64},{96,112},{112,96},{1... | collective-permute-start | bytes 589832 | tf_op jit(solution)/shard_map/ppermute | solution.py:330
  90.1 0.0 collective-permute-done.3.refs_1_
  90.1 2.0 %collective-permute-start.7 = (bf16[384,256]{1,0:T(8,128)(2,1)S(1)}, bf16[384,256]{1,0:T(8,128)(2,1)S(1)}, u32[]{:S(2)}, u32[]{:S(2)}) collective-permute-start(bf16[384,256]{1,0:T(8,128)(2,1)S(1)} %collective-permute-done.3.refs_1_), channel_id=1, source_target_pairs={{0,16},{16,0},{32,48},{48,32},{64,80},{80,64},{96,112},{112,96},{1... | collective-permute-start | bytes 589832 | tf_op jit(solution)/shard_map/ppermute | solution.py:330
  92.1 0.0 collective-permute-done.6.refs_4_
  92.1 0.0 collective-permute-done.9.refs_7_
  92.1 0.0 collective-permute-done.8.refs_6_
  92.1 1.1 %collective-permute-done.7.refs_5_ = bf16[384,256]{1,0:T(8,128)(2,1)S(1)} collective-permute-done((bf16[384,256]{1,0:T(8,128)(2,1)S(1)}, bf16[384,256]{1,0:T(8,128)(2,1)S(1)}, u32[]{:S(2)}, u32[]{:S(2)}) %collective-permute-start.7) | collective-permute-done | bytes 196640 | tf_op jit(solution)/shard_map/ppermute | solution.py:330
  93.2 1.2 %update.1 = f32[48,32,256]{2,1,0:T(8,128)} custom-call(s32[1]{0:T(128)} %bitcast.4.layer, f32[48,32,256]{2,1,0:T(8,128)S(1)} %bring.1.factors, bf16[384,256]{1,0:T(8,128)(2,1)S(1)} %add.2.ready.refs_0_, bf16[384,256]{1,0:T(8,128)(2,1)S(1)} %collective-permute-done.3.refs_1_, bf16[384,256]{1,0:T(8,128)(2,1)S(1)} %collective-permute-done.4.refs_2_, ...), custom_call_target="tpu_custom_call" | custom-call | tf_op jit(solution)/shard_map/update/pallas_call | solution.py:332
  (2 shorter events, 0.0 us)
Async XLA Ops:
  2.2 14.2 %all-to-all-start = ((s32[16,8,128]{2,1,0:T(8,128)}), s32[16,8,128]{2,1,0:T(8,128)S(1)}, u32[]{:S(2)}, u32[]{:S(2)}) async-start(s32[16,8,128]{2,1,0:T(8,128)} %get-tuple-element.20), calls=%async_computation | async-start | bytes 131072 | tf_op jit(solution)/shard_map/all_to_all | solution.py:243
  11.9 24.9 %copy-start = (s32[32]{0:T(128)S(1)}, s32[32]{0:T(128)}, u32[]{:S(2)}) copy-start(s32[32]{0:T(128)} %get-tuple-element.28.slots) | copy-start | bytes 388
  18.1 18.7 %all-to-all-start.1 = ((bf16[16,128,256]{2,1,0:T(8,128)(2,1)}), bf16[16,128,256]{2,1,0:T(8,128)(2,1)S(1)}, u32[]{:S(2)}, u32[]{:S(2)}) async-start(bf16[16,128,256]{2,1,0:T(8,128)(2,1)} %get-tuple-element.29), calls=%async_computation.1 | async-start | bytes 2097152 | tf_op jit(solution)/shard_map/all_to_all | solution.py:271
  21.8 4.5 %collective-permute-start.2 = (s32[8,128]{1,0:T(8,128)S(1)}, s32[8,128]{1,0:T(8,128)S(1)}, u32[]{:S(2)}, u32[]{:S(2)}) collective-permute-start(s32[8,128]{1,0:T(8,128)S(1)} %get-tuple-element.24.table_0), channel_id=1, source_target_pairs={{0,96},{16,112},{32,0},{48,16},{64,32},{80,48},{96,64},{112,80},{1... | collective-permute-start | bytes 12296 | tf_op jit(solution)/shard_map/ppermute | solution.py:277
  25.5 4.0 %collective-permute-start.1 = (s32[8,128]{1,0:T(8,128)S(1)}, s32[8,128]{1,0:T(8,128)S(1)}, u32[]{:S(2)}, u32[]{:S(2)}) collective-permute-start(s32[8,128]{1,0:T(8,128)S(1)} %get-tuple-element.24.table_0), channel_id=1, source_target_pairs={{0,64},{16,80},{32,96},{48,112},{64,0},{80,16},{96,32},{112,48},{1... | collective-permute-start | bytes 12296 | tf_op jit(solution)/shard_map/ppermute | solution.py:277
  25.5 4.0 %collective-permute-start = (s32[8,128]{1,0:T(8,128)S(1)}, s32[8,128]{1,0:T(8,128)S(1)}, u32[]{:S(2)}, u32[]{:S(2)}) collective-permute-start(s32[8,128]{1,0:T(8,128)S(1)} %get-tuple-element.24.table_0), channel_id=1, source_target_pairs={{0,32},{16,48},{32,64},{48,80},{64,96},{80,112},{96,0},{112,16},{1... | collective-permute-start | bytes 12296 | tf_op jit(solution)/shard_map/ppermute | solution.py:277
  77.8 8.2 %collective-permute-start.5 = (bf16[384,256]{1,0:T(8,128)(2,1)S(1)}, bf16[384,256]{1,0:T(8,128)(2,1)S(1)}, u32[]{:S(2)}, u32[]{:S(2)}) collective-permute-start(bf16[384,256]{1,0:T(8,128)(2,1)S(1)} %add.2.ready.refs_0_), channel_id=1, source_target_pairs={{0,96},{16,112},{32,0},{48,16},{64,32},{80,48},{96,64},{112,80},{1... | collective-permute-start | bytes 589832 | tf_op jit(solution)/shard_map/ppermute | solution.py:317
  78.5 9.2 %collective-permute-start.4 = (bf16[384,256]{1,0:T(8,128)(2,1)S(1)}, bf16[384,256]{1,0:T(8,128)(2,1)S(1)}, u32[]{:S(2)}, u32[]{:S(2)}) collective-permute-start(bf16[384,256]{1,0:T(8,128)(2,1)S(1)} %add.2.ready.refs_0_), channel_id=1, source_target_pairs={{0,64},{16,80},{32,96},{48,112},{64,0},{80,16},{96,32},{112,48},{1... | collective-permute-start | bytes 589832 | tf_op jit(solution)/shard_map/ppermute | solution.py:317
  79.4 10.7 %collective-permute-start.3 = (bf16[384,256]{1,0:T(8,128)(2,1)S(1)}, bf16[384,256]{1,0:T(8,128)(2,1)S(1)}, u32[]{:S(2)}, u32[]{:S(2)}) collective-permute-start(bf16[384,256]{1,0:T(8,128)(2,1)S(1)} %add.2.ready.refs_0_), channel_id=1, source_target_pairs={{0,32},{16,48},{32,64},{48,80},{64,96},{80,112},{96,0},{112,16},{1... | collective-permute-start | bytes 589832 | tf_op jit(solution)/shard_map/ppermute | solution.py:317
  80.8 11.3 %collective-permute-start.6 = (bf16[384,256]{1,0:T(8,128)(2,1)S(1)}, bf16[384,256]{1,0:T(8,128)(2,1)S(1)}, u32[]{:S(2)}, u32[]{:S(2)}) collective-permute-start(bf16[384,256]{1,0:T(8,128)(2,1)S(1)} %add.2.ready.refs_0_), channel_id=1, source_target_pairs={{0,16},{16,0},{32,48},{48,32},{64,80},{80,64},{96,112},{112,96},{1... | collective-permute-start | bytes 589832 | tf_op jit(solution)/shard_map/ppermute | solution.py:330
  86.0 6.1 %collective-permute-start.9 = (bf16[384,256]{1,0:T(8,128)(2,1)S(1)}, bf16[384,256]{1,0:T(8,128)(2,1)S(1)}, u32[]{:S(2)}, u32[]{:S(2)}) collective-permute-start(bf16[384,256]{1,0:T(8,128)(2,1)S(1)} %collective-permute-done.5.refs_3_), channel_id=1, source_target_pairs={{0,16},{16,0},{32,48},{48,32},{64,80},{80,64},{96,112},{112,96},{1... | collective-permute-start | bytes 589832 | tf_op jit(solution)/shard_map/ppermute | solution.py:330
  87.7 4.4 %collective-permute-start.8 = (bf16[384,256]{1,0:T(8,128)(2,1)S(1)}, bf16[384,256]{1,0:T(8,128)(2,1)S(1)}, u32[]{:S(2)}, u32[]{:S(2)}) collective-permute-start(bf16[384,256]{1,0:T(8,128)(2,1)S(1)} %collective-permute-done.4.refs_2_), channel_id=1, source_target_pairs={{0,16},{16,0},{32,48},{48,32},{64,80},{80,64},{96,112},{112,96},{1... | collective-permute-start | bytes 589832 | tf_op jit(solution)/shard_map/ppermute | solution.py:330
  90.1 3.1 %collective-permute-start.7 = (bf16[384,256]{1,0:T(8,128)(2,1)S(1)}, bf16[384,256]{1,0:T(8,128)(2,1)S(1)}, u32[]{:S(2)}, u32[]{:S(2)}) collective-permute-start(bf16[384,256]{1,0:T(8,128)(2,1)S(1)} %collective-permute-done.3.refs_1_), channel_id=1, source_target_pairs={{0,16},{16,0},{32,48},{48,32},{64,80},{80,64},{96,112},{112,96},{1... | collective-permute-start | bytes 589832 | tf_op jit(solution)/shard_map/ppermute | solution.py:330

commit v5 on v4

--- a/solution.py
+++ b/solution.py
@@ -198,7 +198,7 @@
     total[...] = summed.reshape(total.shape).astype(total.dtype)
 
 
-def update_kernel(layer, factors, *refs):
+def update_kernel(order, layer, factors, *refs):
     own, other, (out, stepped, sems) = refs[:4], refs[4:8], refs[8:]
     parts = len(own)
     height = TILE // parts
@@ -207,10 +207,10 @@
     for mode in range(4):
         blocks = slice(mode * held, (mode + 1) * held)
         lines = slice(mode * held * height, (mode + 1) * held * height)
-        for back in range(parts):
+        for back, mine, theirs in zip(order, own, other):
             source = lax.rem(layer[0] + parts - back, parts)
             at = pl.ds(pl.multiple_of(source * height, height), height)
-            gradient = own[back][lines, :].astype(jnp.float32) + other[back][lines, :].astype(jnp.float32)
+            gradient = mine[lines, :].astype(jnp.float32) + theirs[lines, :].astype(jnp.float32)
             gradient = gradient.reshape(held, height, -1)
             stepped[blocks, at, :] = factors[blocks, at, :] - step_size * gradient
         copies.append(pltpu.make_async_copy(stepped.at[blocks], out.at[blocks], sems.at[mode]))
@@ -314,7 +314,8 @@
         name="add",
     )(layer, *tables, in_vmem(came))
 
-    own = [partial] + [lax.ppermute(partial, "tiles", round_trip(back)) for back in range(1, layers)]
+    order = [0] + sorted(range(1, layers), key=lambda back: -min(back, layers - back))
+    own = [partial] + [lax.ppermute(partial, "tiles", round_trip(back)) for back in order[1:]]
     pair = [(i, i ^ 1) for i in range(2 * layers)]
     kept = pl.pallas_call(
         bring_kernel,
@@ -330,7 +331,7 @@
     other = [lax.ppermute(piece, "tiles", pair) for piece in [here] + own[1:]]
 
     updated = pl.pallas_call(
-        update_kernel,
+        functools.partial(update_kernel, order),
         out_shape=jax.ShapeDtypeStruct(factor_blocks.shape, f32),
         in_specs=[SMEM] + [VMEM] * 9,
         out_specs=ANY,

time: 96 us -> 96.4 us (level); the launches traced: 94.4 us -> 97.7 us
  blocking collectives: 30.6 us -> 34.8 us
    all_to_all x1, blocking collectives: 30.6 us -> 34.8 us  [on_device(): lax.all_to_all(messages, ('tiles', 'rows'), 0, 0, axis_index_groups=same_...]
    ppermute x4, starting transfers between devices: 11.3 us -> 9.91 us  [on_device(): other = [lax.ppermute(piece, 'tiles', pair) for piece in [here] + own[1:]]]
  transfers between devices with their start and end apart: 12 -> 12, of which waited for: 4 -> 6; matrix products, arithmetic and copies ran while one was open for 0% -> 0% of each run, Pallas kernels for 4% -> 4%
where the time goes in v5:
time: 96.4 us; the launch traced here: 97.7 us
  blocking collectives  34.8 us (36%)
  starting transfers between devices  27.9 us (29%)
  Pallas kernels  18.3 us (19%)
  waiting for transfers between devices  16 us (17%)
    all_to_all x1, blocking collectives, on_device(): lax.all_to_all(messages, ('tiles', 'rows'), 0, 0, axis_index_groups=same_...  34.8 us
    ppermute x4, starting transfers between devices, on_device(): other = [lax.ppermute(piece, 'tiles', pair) for piece in [here] + own[1:]]  9.91 us
    pallas_call x1, Pallas kernels, on_device(): pl.pallas_call(functools.partial(tile_kernel, owners, layers, 256), out_s...  8.87 us
    all_to_all x1, starting transfers between devices, on_device(): asked = lax.all_to_all(wanted, 'rows', 0, 0)  7.6 us
    all_to_all x1, waiting for transfers between devices, on_device(): lax.all_to_all(sent, 'rows', 0, 0).reshape(owners * CAP * TILE, rank)  6.86 us
    ppermute x3, starting transfers between devices, on_device(): lax.ppermute(table, 'tiles', round_trip(back))  4.69 us
    all_to_all x1, waiting for transfers between devices, on_device(): asked = lax.all_to_all(wanted, 'rows', 0, 0)  4.41 us
    all_to_all x1, starting transfers between devices, on_device(): lax.all_to_all(sent, 'rows', 0, 0).reshape(owners * CAP * TILE, rank)  3.67 us
  transfers between devices with their start and end apart: 12, of which 6 were waited for; matrix products, arithmetic and copies ran while one was open for 0% of the time, Pallas kernels for 4%

profile of v5, /device:TPU:1, one launch (start us, length us, event | category | flops | bytes accessed | tf_op | source)
XLA Modules:
  0.0 97.7 jit_solution(1502284954082875371)
XLA Ops:
  0.7 1.5 %requests.1 = (s32[16,8,128]{2,1,0:T(8,128)}, s32[32]{0:T(128)}) custom-call(s32[4,8]{1,0:T(4,128)} %bitcast.13, s32[1]{0:T(128)S(6)} %copy.5.count), custom_call_target="tpu_custom_call" | custom-call | tf_op jit(solution)/shard_map/requests/pallas_call | solution.py:232
  2.2 7.6 %all-to-all-start = ((s32[16,8,128]{2,1,0:T(8,128)}), s32[16,8,128]{2,1,0:T(8,128)S(1)}, u32[]{:S(2)}, u32[]{:S(2)}) async-start(s32[16,8,128]{2,1,0:T(8,128)} %get-tuple-element.20), calls=%async_computation | async-start | bytes 131072 | tf_op jit(solution)/shard_map/all_to_all | solution.py:243
  9.8 2.1 %prepare.1 = (bf16[48,32,256]{2,1,0:T(8,128)(2,1)S(1)}, bf16[1024,1024]{1,0:T(8,128)(2,1)S(1)}) custom-call(f32[48,32,256]{2,1,0:T(8,128)} %bitcast.11, bf16[8,1024,1024]{2,1,0:T(8,128)(2,1)} %bitcast.9), custom_call_target="tpu_custom_call" | custom-call | bytes 4194304 | tf_op jit(solution)/shard_map/prepare/pallas_call | solution.py:245
  11.9 4.4 %all-to-all-done.asked = s32[16,8,128]{2,1,0:T(8,128)S(1)} async-done(((s32[16,8,128]{2,1,0:T(8,128)}), s32[16,8,128]{2,1,0:T(8,128)S(1)}, u32[]{:S(2)}, u32[]{:S(2)}) %all-to-all-start) | async-done | bytes 65568 | tf_op jit(solution)/shard_map/all_to_all | solution.py:243
  16.3 1.7 %serve.1 = (bf16[16,128,256]{2,1,0:T(8,128)(2,1)}, s32[8,128]{1,0:T(8,128)S(1)}) custom-call(s32[16,8,128]{2,1,0:T(8,128)S(1)} %all-to-all-done.asked, bf16[48,32,256]{2,1,0:T(8,128)(2,1)S(1)} %get-tuple-element.21.narrow), custom_call_target="tpu_custom_call" | custom-call | tf_op jit(solution)/shard_map/serve/pallas_call | solution.py:255
  18.0 3.7 %all-to-all-start.1 = ((bf16[16,128,256]{2,1,0:T(8,128)(2,1)}), bf16[16,128,256]{2,1,0:T(8,128)(2,1)S(1)}, u32[]{:S(2)}, u32[]{:S(2)}) async-start(bf16[16,128,256]{2,1,0:T(8,128)(2,1)} %get-tuple-element.29), calls=%async_computation.1 | async-start | bytes 2097152 | tf_op jit(solution)/shard_map/all_to_all | solution.py:271
  21.7 4.0 %collective-permute-start.2 = (s32[8,128]{1,0:T(8,128)S(1)}, s32[8,128]{1,0:T(8,128)S(1)}, u32[]{:S(2)}, u32[]{:S(2)}) collective-permute-start(s32[8,128]{1,0:T(8,128)S(1)} %get-tuple-element.24.table_0), channel_id=1, source_target_pairs={{0,96},{16,112},{32,0},{48,16},{64,32},{80,48},{96,64},{112,80},{1... | collective-permute-start | bytes 12296 | tf_op jit(solution)/shard_map/ppermute | solution.py:277
  25.7 0.0 collective-permute-start.1
  25.7 0.7 collective-permute-start
  26.3 0.1 collective-permute-done.2.table_3
  26.4 3.2 %collective-permute-done.1.table_2 = s32[8,128]{1,0:T(8,128)S(1)} collective-permute-done((s32[8,128]{1,0:T(8,128)S(1)}, s32[8,128]{1,0:T(8,128)S(1)}, u32[]{:S(2)}, u32[]{:S(2)}) %collective-permute-start.1) | collective-permute-done | bytes 4128 | tf_op jit(solution)/shard_map/ppermute | solution.py:277
  29.6 0.0 collective-permute-done.table_1
  29.6 6.9 %all-to-all-done.1 = bf16[16,128,256]{2,1,0:T(8,128)(2,1)S(1)} async-done(((bf16[16,128,256]{2,1,0:T(8,128)(2,1)}), bf16[16,128,256]{2,1,0:T(8,128)(2,1)S(1)}, u32[]{:S(2)}, u32[]{:S(2)}) %all-to-all-start.1) | async-done | bytes 1048608 | tf_op jit(solution)/shard_map/all_to_all | solution.py:271
  36.5 8.9 %tiles.1 = bf16[64,32,256]{2,1,0:T(8,128)(2,1)S(1)} custom-call(s32[1]{0:T(128)S(6)} %copy.5.count, s32[32]{0:T(128)S(1)} %copy-done, bf16[2048,256]{1,0:T(8,128)(2,1)S(1)} %bitcast.8, bf16[1024,1024]{1,0:T(8,128)(2,1)S(1)} %get-tuple-element.30.early, bf16[8,1024,1024]{2,1,0:T(8,128)(2,1)} %bitcast.10), custom_call_target="tpu_custom_call" | custom-call | flops 12884901888 | bytes 16777216 | tf_op jit(solution)/shard_map/tiles/pallas_call | solution.py:281
  45.4 34.8 %all_to_all.15.came = bf16[64,32,256]{2,1,0:T(8,128)(2,1)S(1)} all-to-all(bf16[64,32,256]{2,1,0:T(8,128)(2,1)S(1)} %tiles.1), channel_id=1, replica_groups={{0,1,2,3,4,5,6,7,8,9,10,11,12,13,14,15,32,33,34,35,36,37,38,39,40,41,42..., dimensions={0} | all-to-all | bytes 2097152 | tf_op jit(solution)/shard_map/all_to_all | solution.py:304
  80.2 1.5 %add.2.ready.refs_0_ = bf16[384,256]{1,0:T(8,128)(2,1)S(1)} custom-call(s32[1]{0:T(128)} %bitcast.4.layer, s32[8,128]{1,0:T(8,128)S(1)} %get-tuple-element.24.table_0, s32[8,128]{1,0:T(8,128)S(1)} %collective-permute-done.table_1, s32[8,128]{1,0:T(8,128)S(1)} %collective-permute-done.1.table_2, s32[8,128]{1,0:T(8,128)S(1)} %collective-permute-done.2.table_3, ...), custom_call_target="tpu_custom_call" | custom-call | tf_op jit(solution)/shard_map/add/pallas_call | solution.py:307
  81.7 0.6 collective-permute-start.5
  82.3 0.9 collective-permute-start.4
  83.2 0.5 collective-permute-start.3
  83.7 1.4 %bring.1.factors = f32[48,32,256]{2,1,0:T(8,128)S(1)} custom-call(bf16[384,256]{1,0:T(8,128)(2,1)S(1)} %add.2.ready.refs_0_, f32[48,32,256]{2,1,0:T(8,128)} %bitcast.12), custom_call_target="tpu_custom_call" | custom-call | bytes 4194304 | tf_op jit(solution)/shard_map/bring/pallas_call | solution.py:320
  85.1 3.2 %collective-permute-start.6 = (bf16[384,256]{1,0:T(8,128)(2,1)S(1)}, bf16[384,256]{1,0:T(8,128)(2,1)S(1)}, u32[]{:S(2)}, u32[]{:S(2)}) collective-permute-start(bf16[384,256]{1,0:T(8,128)(2,1)S(1)} %add.2.ready.refs_0_), channel_id=1, source_target_pairs={{0,16},{16,0},{32,48},{48,32},{64,80},{80,64},{96,112},{112,96},{1... | collective-permute-start | bytes 589832 | tf_op jit(solution)/shard_map/ppermute | solution.py:331
  88.3 0.0 collective-permute-done.5.refs_3_
  88.3 3.1 %collective-permute-start.9 = (bf16[384,256]{1,0:T(8,128)(2,1)S(1)}, bf16[384,256]{1,0:T(8,128)(2,1)S(1)}, u32[]{:S(2)}, u32[]{:S(2)}) collective-permute-start(bf16[384,256]{1,0:T(8,128)(2,1)S(1)} %collective-permute-done.5.refs_3_), channel_id=1, source_target_pairs={{0,16},{16,0},{32,48},{48,32},{64,80},{80,64},{96,112},{112,96},{1... | collective-permute-start | bytes 589832 | tf_op jit(solution)/shard_map/ppermute | solution.py:331
  91.4 0.0 collective-permute-done.4.refs_2_
  91.4 3.6 %collective-permute-start.8 = (bf16[384,256]{1,0:T(8,128)(2,1)S(1)}, bf16[384,256]{1,0:T(8,128)(2,1)S(1)}, u32[]{:S(2)}, u32[]{:S(2)}) collective-permute-start(bf16[384,256]{1,0:T(8,128)(2,1)S(1)} %collective-permute-done.4.refs_2_), channel_id=1, source_target_pairs={{0,16},{16,0},{32,48},{48,32},{64,80},{80,64},{96,112},{112,96},{1... | collective-permute-start | bytes 589832 | tf_op jit(solution)/shard_map/ppermute | solution.py:331
  95.0 0.0 collective-permute-done.3.refs_1_
  95.0 0.0 collective-permute-start.7
  95.0 0.0 collective-permute-done.6.refs_4_
  95.0 0.0 collective-permute-done.9.refs_7_
  95.1 1.0 %collective-permute-done.8.refs_6_ = bf16[384,256]{1,0:T(8,128)(2,1)S(1)} collective-permute-done((bf16[384,256]{1,0:T(8,128)(2,1)S(1)}, bf16[384,256]{1,0:T(8,128)(2,1)S(1)}, u32[]{:S(2)}, u32[]{:S(2)}) %collective-permute-start.8) | collective-permute-done | bytes 196640 | tf_op jit(solution)/shard_map/ppermute | solution.py:331
  96.1 0.4 collective-permute-done.7.refs_5_
  96.5 1.2 %update.1 = f32[48,32,256]{2,1,0:T(8,128)} custom-call(s32[1]{0:T(128)} %bitcast.4.layer, f32[48,32,256]{2,1,0:T(8,128)S(1)} %bring.1.factors, bf16[384,256]{1,0:T(8,128)(2,1)S(1)} %add.2.ready.refs_0_, bf16[384,256]{1,0:T(8,128)(2,1)S(1)} %collective-permute-done.3.refs_1_, bf16[384,256]{1,0:T(8,128)(2,1)S(1)} %collective-permute-done.4.refs_2_, ...), custom_call_target="tpu_custom_call" | custom-call | tf_op jit(solution)/shard_map/update/pallas_call | solution.py:333
  (2 shorter events, 0.0 us)
Async XLA Ops:
  2.2 14.1 %all-to-all-start = ((s32[16,8,128]{2,1,0:T(8,128)}), s32[16,8,128]{2,1,0:T(8,128)S(1)}, u32[]{:S(2)}, u32[]{:S(2)}) async-start(s32[16,8,128]{2,1,0:T(8,128)} %get-tuple-element.20), calls=%async_computation | async-start | bytes 131072 | tf_op jit(solution)/shard_map/all_to_all | solution.py:243
  11.9 24.6 %copy-start = (s32[32]{0:T(128)S(1)}, s32[32]{0:T(128)}, u32[]{:S(2)}) copy-start(s32[32]{0:T(128)} %get-tuple-element.28.slots) | copy-start | bytes 388
  18.0 18.5 %all-to-all-start.1 = ((bf16[16,128,256]{2,1,0:T(8,128)(2,1)}), bf16[16,128,256]{2,1,0:T(8,128)(2,1)S(1)}, u32[]{:S(2)}, u32[]{:S(2)}) async-start(bf16[16,128,256]{2,1,0:T(8,128)(2,1)} %get-tuple-element.29), calls=%async_computation.1 | async-start | bytes 2097152 | tf_op jit(solution)/shard_map/all_to_all | solution.py:271
  21.7 4.8 %collective-permute-start.2 = (s32[8,128]{1,0:T(8,128)S(1)}, s32[8,128]{1,0:T(8,128)S(1)}, u32[]{:S(2)}, u32[]{:S(2)}) collective-permute-start(s32[8,128]{1,0:T(8,128)S(1)} %get-tuple-element.24.table_0), channel_id=1, source_target_pairs={{0,96},{16,112},{32,0},{48,16},{64,32},{80,48},{96,64},{112,80},{1... | collective-permute-start | bytes 12296 | tf_op jit(solution)/shard_map/ppermute | solution.py:277
  25.7 4.0 %collective-permute-start.1 = (s32[8,128]{1,0:T(8,128)S(1)}, s32[8,128]{1,0:T(8,128)S(1)}, u32[]{:S(2)}, u32[]{:S(2)}) collective-permute-start(s32[8,128]{1,0:T(8,128)S(1)} %get-tuple-element.24.table_0), channel_id=1, source_target_pairs={{0,64},{16,80},{32,96},{48,112},{64,0},{80,16},{96,32},{112,48},{1... | collective-permute-start | bytes 12296 | tf_op jit(solution)/shard_map/ppermute | solution.py:277
  25.7 4.0 %collective-permute-start = (s32[8,128]{1,0:T(8,128)S(1)}, s32[8,128]{1,0:T(8,128)S(1)}, u32[]{:S(2)}, u32[]{:S(2)}) collective-permute-start(s32[8,128]{1,0:T(8,128)S(1)} %get-tuple-element.24.table_0), channel_id=1, source_target_pairs={{0,32},{16,48},{32,64},{48,80},{64,96},{80,112},{96,0},{112,16},{1... | collective-permute-start | bytes 12296 | tf_op jit(solution)/shard_map/ppermute | solution.py:277
  81.7 6.7 %collective-permute-start.5 = (bf16[384,256]{1,0:T(8,128)(2,1)S(1)}, bf16[384,256]{1,0:T(8,128)(2,1)S(1)}, u32[]{:S(2)}, u32[]{:S(2)}) collective-permute-start(bf16[384,256]{1,0:T(8,128)(2,1)S(1)} %add.2.ready.refs_0_), channel_id=1, source_target_pairs={{0,96},{16,112},{32,0},{48,16},{64,32},{80,48},{96,64},{112,80},{1... | collective-permute-start | bytes 589832 | tf_op jit(solution)/shard_map/ppermute | solution.py:318
  82.3 9.1 %collective-permute-start.4 = (bf16[384,256]{1,0:T(8,128)(2,1)S(1)}, bf16[384,256]{1,0:T(8,128)(2,1)S(1)}, u32[]{:S(2)}, u32[]{:S(2)}) collective-permute-start(bf16[384,256]{1,0:T(8,128)(2,1)S(1)} %add.2.ready.refs_0_), channel_id=1, source_target_pairs={{0,32},{16,48},{32,64},{48,80},{64,96},{80,112},{96,0},{112,16},{1... | collective-permute-start | bytes 589832 | tf_op jit(solution)/shard_map/ppermute | solution.py:318
  83.2 11.8 %collective-permute-start.3 = (bf16[384,256]{1,0:T(8,128)(2,1)S(1)}, bf16[384,256]{1,0:T(8,128)(2,1)S(1)}, u32[]{:S(2)}, u32[]{:S(2)}) collective-permute-start(bf16[384,256]{1,0:T(8,128)(2,1)S(1)} %add.2.ready.refs_0_), channel_id=1, source_target_pairs={{0,64},{16,80},{32,96},{48,112},{64,0},{80,16},{96,32},{112,48},{1... | collective-permute-start | bytes 589832 | tf_op jit(solution)/shard_map/ppermute | solution.py:318
  85.1 9.9 %collective-permute-start.6 = (bf16[384,256]{1,0:T(8,128)(2,1)S(1)}, bf16[384,256]{1,0:T(8,128)(2,1)S(1)}, u32[]{:S(2)}, u32[]{:S(2)}) collective-permute-start(bf16[384,256]{1,0:T(8,128)(2,1)S(1)} %add.2.ready.refs_0_), channel_id=1, source_target_pairs={{0,16},{16,0},{32,48},{48,32},{64,80},{80,64},{96,112},{112,96},{1... | collective-permute-start | bytes 589832 | tf_op jit(solution)/shard_map/ppermute | solution.py:331
  88.3 6.7 %collective-permute-start.9 = (bf16[384,256]{1,0:T(8,128)(2,1)S(1)}, bf16[384,256]{1,0:T(8,128)(2,1)S(1)}, u32[]{:S(2)}, u32[]{:S(2)}) collective-permute-start(bf16[384,256]{1,0:T(8,128)(2,1)S(1)} %collective-permute-done.5.refs_3_), channel_id=1, source_target_pairs={{0,16},{16,0},{32,48},{48,32},{64,80},{80,64},{96,112},{112,96},{1... | collective-permute-start | bytes 589832 | tf_op jit(solution)/shard_map/ppermute | solution.py:331
  91.4 4.7 %collective-permute-start.8 = (bf16[384,256]{1,0:T(8,128)(2,1)S(1)}, bf16[384,256]{1,0:T(8,128)(2,1)S(1)}, u32[]{:S(2)}, u32[]{:S(2)}) collective-permute-start(bf16[384,256]{1,0:T(8,128)(2,1)S(1)} %collective-permute-done.4.refs_2_), channel_id=1, source_target_pairs={{0,16},{16,0},{32,48},{48,32},{64,80},{80,64},{96,112},{112,96},{1... | collective-permute-start | bytes 589832 | tf_op jit(solution)/shard_map/ppermute | solution.py:331
  95.0 1.4 %collective-permute-start.7 = (bf16[384,256]{1,0:T(8,128)(2,1)S(1)}, bf16[384,256]{1,0:T(8,128)(2,1)S(1)}, u32[]{:S(2)}, u32[]{:S(2)}) collective-permute-start(bf16[384,256]{1,0:T(8,128)(2,1)S(1)} %collective-permute-done.3.refs_1_), channel_id=1, source_target_pairs={{0,16},{16,0},{32,48},{48,32},{64,80},{80,64},{96,112},{112,96},{1... | collective-permute-start | bytes 589832 | tf_op jit(solution)/shard_map/ppermute | solution.py:331
